TPU v7x, 128 devices: a whole 4x4x4 slice. The times are simulated.
128 devices in a mesh: dp: 2 (over core), row: 8 (over x_lo, y), col: 8 (over z, x_hi).
Axes of the slice: x: 4 (x_hi: 2, x_lo: 2; x = x_hi * 2 + x_lo), y: 4, z: 4, core: 2. Of those that a mesh axis runs over, the one named last changes fastest.
Arguments:
- hidden: bfloat16 [2048, 28672], P(('dp', 'col'), 'row'), may hold values from -0.1875 to 0.1875
- cotangent: bfloat16 [2048, 8192], P(('dp', 'row'), 'col'), may hold values from -6 to 6
- language: int32 [2048], P(('dp', 'row')), may hold values from 0 to 31
- counts: int32 [32], replicated, may hold values from 128 to 2047
- weight: bfloat16 [28672, 8192], P('row', 'col'), may hold values from -0.0625 to 0.0625
Outputs:
- grad_hidden: bfloat16 [2048, 28672], P(('dp', 'col'), 'row')
- grad_weight: float32 [28672, 8192], P('row', ('col', 'dp'))
All inputs are finite; a program needn't handle non-finite values.
Results may differ from a plain program's by a relative error of at most 0.013.
Values may be sent and summed in bfloat16 or wider, within the bound.
A program may use at most 256 MiB of HBM per device.

v0:
```python
import jax
import jax.numpy as jnp
from jax import lax
from jax.sharding import PartitionSpec as P


def shifted_2(array, axis, by):
    devices = lax.axis_size(axis)
    return lax.ppermute(array, axis, [(i, (i + by) % devices) for i in range(devices)])


def token_scale(cotangent, language, counts):
    lang_weight = jnp.sqrt(512.0 / counts.astype(jnp.float32))
    matches = language[:, None] == jnp.arange(counts.shape[0], dtype=jnp.int32)[None, :]
    token_weight = jnp.sum(jnp.where(matches, lang_weight[None, :], 0.0), axis=1)
    return (cotangent.astype(jnp.float32) * token_weight[:, None]).astype(jnp.bfloat16)


def body(hidden, cotangent, language, counts, weight):
    scaled = token_scale(cotangent, language, counts)
    block_tokens = hidden.shape[0]
    grid_size = lax.axis_size("row")
    bit_count = (grid_size - 1).bit_length()
    row_at = lax.axis_index("row")
    col_at = lax.axis_index("col")
    moving_hidden = hidden
    moving_cotan = scaled
    for bit_pos in range(bit_count):
        shifted = shifted_2(moving_hidden, "col", -(1 << bit_pos))
        moving_hidden = jnp.where(row_at >> bit_pos & 1 == 1, shifted, moving_hidden)
        moved = shifted_2(moving_cotan, "row", -(1 << bit_pos))
        moving_cotan = jnp.where(col_at >> bit_pos & 1 == 1, moved, moving_cotan)
    weight_grad = jnp.zeros((weight.shape[0], weight.shape[1]), jnp.float32)
    partial_value = jnp.zeros((block_tokens, weight.shape[0]), jnp.float32)
    for section in range(grid_size):
        weight_grad = weight_grad + lax.dot_general(
            moving_hidden,
            moving_cotan,
            (((0,), (0,)), ((), ())),
            preferred_element_type=jnp.float32,
        )
        partial_value = partial_value + lax.dot_general(
            moving_cotan, weight, (((1,), (1,)), ((), ())), preferred_element_type=jnp.float32
        )
        partial_value = shifted_2(partial_value.astype(jnp.bfloat16), "col", -1).astype(
            partial_value.dtype
        )
        if section + 1 < grid_size:
            moving_hidden = shifted_2(moving_hidden, "col", -1)
            moving_cotan = shifted_2(moving_cotan, "row", -1)
    finished = partial_value.astype(jnp.bfloat16)
    for bit_pos in range(bit_count):
        returned = shifted_2(finished, "col", 1 << bit_pos)
        finished = jnp.where(row_at >> bit_pos & 1 == 1, returned, finished)
    grad_weight = lax.psum_scatter(
        weight_grad.astype(jnp.bfloat16), "dp", scatter_dimension=1, tiled=True
    ).astype(jnp.float32)
    return (finished, grad_weight)


def solution(mesh):
    placed = (
        P(("dp", "col"), "row"),
        P(("dp", "row"), "col"),
        P(("dp", "row")),
        P(),
        P("row", "col"),
    )
    return jax.shard_map(
        body,
        mesh=mesh,
        in_specs=placed,
        out_specs=(P(("dp", "col"), "row"), P("row", ("col", "dp"))),
        check_vma=False,
    )
```

profile of v0, /device:TPU:2, one launch (start us, length us, event | category | flops | bytes accessed | tf_op | source)
XLA Modules:
  0.0 604.4 jit_solution(12982353932358102161)
XLA Ops:
  12.9 19.9 %collective-permute-done.21 = bf16[128,3584]{1,0:T(8,128)(2,1)S(1)} collective-permute-done((bf16[128,3584]{1,0:T(8,128)(2,1)}, bf16[128,3584]{1,0:T(8,128)(2,1)S(1)}, u32[]{:S(2)}, u32[]{:S(2)}) %collective-permute-start.21) | collective-permute-done | bytes 917536 | tf_op jit(solution)/shard_map/ppermute | solution.py:9
  36.5 18.9 %collective-permute-done.22 = bf16[128,3584]{1,0:T(8,128)(2,1)S(1)} collective-permute-done((bf16[128,3584]{1,0:T(8,128)(2,1)S(1)}, bf16[128,3584]{1,0:T(8,128)(2,1)S(1)}, u32[]{:S(2)}, u32[]{:S(2)}) %collective-permute-start.22) | collective-permute-done | bytes 917536 | tf_op jit(solution)/shard_map/ppermute | solution.py:9
  60.0 18.5 %collective-permute-done.23 = bf16[128,3584]{1,0:T(8,128)(2,1)} collective-permute-done((bf16[128,3584]{1,0:T(8,128)(2,1)}, bf16[128,3584]{1,0:T(8,128)(2,1)}, u32[]{:S(2)}, u32[]{:S(2)}) %collective-permute-start.23) | collective-permute-done | bytes 917536 | tf_op jit(solution)/shard_map/ppermute | solution.py:9
  80.7 7.2 %collective-permute-start.24 = (bf16[128,3584]{1,0:T(8,128)(2,1)}, bf16[128,3584]{1,0:T(8,128)(2,1)}, u32[]{:S(2)}, u32[]{:S(2)}) collective-permute-start(bf16[128,3584]{1,0:T(8,128)(2,1)} %broadcast_select_fusion.4), channel_id=1, source_target_pairs={{0,7},{1,0},{2,1},{3,2},{4,3},{5,4},{6,5},{7,6},{8,15},{9,8},{10,9... | collective-permute-start | bytes 2752520 | tf_op jit(solution)/shard_map/ppermute | solution.py:9
  91.4 21.5 %collective-permute-done = bf16[128,1024]{1,0:T(8,128)(2,1)} collective-permute-done((bf16[128,1024]{1,0:T(8,128)(2,1)}, bf16[128,1024]{1,0:T(8,128)(2,1)}, u32[]{:S(2)}, u32[]{:S(2)}) %collective-permute-start) | collective-permute-done | bytes 262176 | tf_op jit(solution)/shard_map/ppermute | solution.py:9
  114.0 7.9 %collective-permute-done.1 = bf16[128,1024]{1,0:T(8,128)(2,1)} collective-permute-done((bf16[128,1024]{1,0:T(8,128)(2,1)}, bf16[128,1024]{1,0:T(8,128)(2,1)}, u32[]{:S(2)}, u32[]{:S(2)}) %collective-permute-start.1) | collective-permute-done | bytes 262176 | tf_op jit(solution)/shard_map/ppermute | solution.py:9
  124.5 21.9 %collective-permute-done.2 = bf16[128,1024]{1,0:T(8,128)(2,1)} collective-permute-done((bf16[128,1024]{1,0:T(8,128)(2,1)S(1)}, bf16[128,1024]{1,0:T(8,128)(2,1)}, u32[]{:S(2)}, u32[]{:S(2)}) %collective-permute-start.2) | collective-permute-done | bytes 262176 | tf_op jit(solution)/shard_map/ppermute | solution.py:9
  146.5 6.4 %collective-permute-done.4 = bf16[128,1024]{1,0:T(8,128)(2,1)S(1)} collective-permute-done((bf16[128,1024]{1,0:T(8,128)(2,1)S(1)}, bf16[128,1024]{1,0:T(8,128)(2,1)S(1)}, u32[]{:S(2)}, u32[]{:S(2)}) %collective-permute-start.4) | collective-permute-done | bytes 262176 | tf_op jit(solution)/shard_map/ppermute | solution.py:9
  167.7 35.8 %collective-permute-done.8 = bf16[128,1024]{1,0:T(8,128)(2,1)S(1)} collective-permute-done((bf16[128,1024]{1,0:T(8,128)(2,1)S(1)}, bf16[128,1024]{1,0:T(8,128)(2,1)S(1)}, u32[]{:S(2)}, u32[]{:S(2)}) %collective-permute-start.8) | collective-permute-done | bytes 262176 | tf_op jit(solution)/shard_map/ppermute | solution.py:9
  218.5 6.8 %collective-permute-done.12 = bf16[128,1024]{1,0:T(8,128)(2,1)S(1)} collective-permute-done((bf16[128,1024]{1,0:T(8,128)(2,1)S(1)}, bf16[128,1024]{1,0:T(8,128)(2,1)S(1)}, u32[]{:S(2)}, u32[]{:S(2)}) %collective-permute-start.12) | collective-permute-done | bytes 262176 | tf_op jit(solution)/shard_map/ppermute | solution.py:9
  241.7 8.5 %fusion.6 = f32[3584,1024]{1,0:T(8,128)} fusion(bf16[128,3584]{1,0:T(8,128)(2,1)} %broadcast_select_fusion.4, bf16[128,1024]{1,0:T(8,128)(2,1)S(1)} %broadcast_select_fusion.8), kind=kOutput, calls=%fused_computation.28 | convolution fusion | flops 939524096 | bytes 15859712 | tf_op jit(solution)/shard_map/dot_general | solution.py:36
  250.2 6.2 %collective-permute-done.27 = bf16[128,3584]{1,0:T(8,128)(2,1)S(1)} collective-permute-done((bf16[128,3584]{1,0:T(8,128)(2,1)S(1)}, bf16[128,3584]{1,0:T(8,128)(2,1)S(1)}, u32[]{:S(2)}, u32[]{:S(2)}) %collective-permute-start.27) | collective-permute-done | bytes 917536 | tf_op jit(solution)/shard_map/ppermute | solution.py:9
  262.4 8.5 %fusion.7 = f32[3584,1024]{1,0:T(8,128)} fusion(bf16[128,3584]{1,0:T(8,128)(2,1)} %collective-permute-done.24, bf16[128,1024]{1,0:T(8,128)(2,1)S(1)} %collective-permute-done.4), kind=kOutput, calls=%fused_computation.29 | convolution fusion | flops 939524096 | bytes 15859712 | tf_op jit(solution)/shard_map/dot_general | solution.py:36
  270.9 8.5 %fusion.8 = f32[3584,1024]{1,0:T(8,128)} fusion(bf16[128,3584]{1,0:T(8,128)(2,1)} %collective-permute-done.25, bf16[128,1024]{1,0:T(8,128)(2,1)S(1)} %collective-permute-done.6), kind=kOutput, calls=%fused_computation.30 | convolution fusion | flops 939524096 | bytes 15859712 | tf_op jit(solution)/shard_map/dot_general | solution.py:36
  279.4 16.8 %collective-permute-done.28 = bf16[128,3584]{1,0:T(8,128)(2,1)S(1)} collective-permute-done((bf16[128,3584]{1,0:T(8,128)(2,1)S(1)}, bf16[128,3584]{1,0:T(8,128)(2,1)S(1)}, u32[]{:S(2)}, u32[]{:S(2)}) %collective-permute-start.28) | collective-permute-done | bytes 917536 | tf_op jit(solution)/shard_map/ppermute | solution.py:9
  301.3 7.3 %fusion.9 = f32[3584,1024]{1,0:T(8,128)} fusion(bf16[128,3584]{1,0:T(8,128)(2,1)S(1)} %collective-permute-done.26, bf16[128,1024]{1,0:T(8,128)(2,1)S(1)} %collective-permute-done.8), kind=kOutput, calls=%fused_computation.31 | convolution fusion | flops 939524096 | bytes 15859712 | tf_op jit(solution)/shard_map/dot_general | solution.py:36
  308.6 7.2 %fusion.10 = f32[3584,1024]{1,0:T(8,128)} fusion(bf16[128,3584]{1,0:T(8,128)(2,1)S(1)} %collective-permute-done.27, bf16[128,1024]{1,0:T(8,128)(2,1)S(1)} %collective-permute-done.10), kind=kOutput, calls=%fused_computation.32 | convolution fusion | flops 939524096 | bytes 15859712 | tf_op jit(solution)/shard_map/dot_general | solution.py:36
  317.3 6.2 %collective-permute-start.30 = (bf16[128,3584]{1,0:T(8,128)(2,1)S(1)}, bf16[128,3584]{1,0:T(8,128)(2,1)S(1)}, u32[]{:S(2)}, u32[]{:S(2)}) collective-permute-start(bf16[128,3584]{1,0:T(8,128)(2,1)S(1)} %collective-permute-done.29), channel_id=1, source_target_pairs={{0,7},{1,0},{2,1},{3,2},{4,3},{5,4},{6,5},{7,6},{8,15},{9,8},{10,9... | collective-permute-start | bytes 2752520 | tf_op jit(solution)/shard_map/ppermute | solution.py:9
  323.6 7.3 %fusion.11 = f32[3584,1024]{1,0:T(8,128)} fusion(bf16[128,3584]{1,0:T(8,128)(2,1)S(1)} %collective-permute-done.28, bf16[128,1024]{1,0:T(8,128)(2,1)S(1)} %collective-permute-done.12), kind=kOutput, calls=%fused_computation.33 | convolution fusion | flops 939524096 | bytes 15859712 | tf_op jit(solution)/shard_map/dot_general | solution.py:36
  330.9 7.2 %fusion.12 = f32[3584,1024]{1,0:T(8,128)} fusion(bf16[128,3584]{1,0:T(8,128)(2,1)S(1)} %collective-permute-done.29, bf16[128,1024]{1,0:T(8,128)(2,1)S(1)} %collective-permute-done.14), kind=kOutput, calls=%fused_computation.34 | convolution fusion | flops 939524096 | bytes 15859712 | tf_op jit(solution)/shard_map/dot_general | solution.py:36
  338.1 35.2 %add_convert_fusion = bf16[3584,1024]{1,0:T(8,128)(2,1)} fusion(f32[3584,1024]{1,0:T(8,128)} %fusion.12, f32[3584,1024]{1,0:T(8,128)} %fusion.11, f32[3584,1024]{1,0:T(8,128)} %fusion.10, f32[3584,1024]{1,0:T(8,128)} %fusion.9, f32[3584,1024]{1,0:T(8,128)} %fusion.8, f32[3584,1024]{1,0:T(8,128)} %fusion.6, f32[3584,1024]{1,0:T(8,128)} %fusion.7, ...), kind=kOutput, calls=%fused_computation | convolution fusion | flops 968884224 | bytes 111280128 | tf_op jit(solution)/shard_map/dot_general | solution.py:36
  381.8 20.9 %collective-permute-done.7 = bf16[128,3584]{1,0:T(8,128)(2,1)S(1)} collective-permute-done((bf16[128,3584]{1,0:T(8,128)(2,1)S(1)}, bf16[128,3584]{1,0:T(8,128)(2,1)S(1)}, u32[]{:S(2)}, u32[]{:S(2)}) %collective-permute-start.7) | collective-permute-done | bytes 917536 | tf_op jit(solution)/shard_map/ppermute | solution.py:9
  406.3 23.2 %collective-permute-done.9 = bf16[128,3584]{1,0:T(8,128)(2,1)S(1)} collective-permute-done((bf16[128,3584]{1,0:T(8,128)(2,1)S(1)}, bf16[128,3584]{1,0:T(8,128)(2,1)S(1)}, u32[]{:S(2)}, u32[]{:S(2)}) %collective-permute-start.9) | collective-permute-done | bytes 917536 | tf_op jit(solution)/shard_map/ppermute | solution.py:9
  432.4 23.8 %collective-permute-done.11 = bf16[128,3584]{1,0:T(8,128)(2,1)S(1)} collective-permute-done((bf16[128,3584]{1,0:T(8,128)(2,1)S(1)}, bf16[128,3584]{1,0:T(8,128)(2,1)S(1)}, u32[]{:S(2)}, u32[]{:S(2)}) %collective-permute-start.11) | collective-permute-done | bytes 917536 | tf_op jit(solution)/shard_map/ppermute | solution.py:9
  459.5 22.4 %collective-permute-done.13 = bf16[128,3584]{1,0:T(8,128)(2,1)S(1)} collective-permute-done((bf16[128,3584]{1,0:T(8,128)(2,1)S(1)}, bf16[128,3584]{1,0:T(8,128)(2,1)S(1)}, u32[]{:S(2)}, u32[]{:S(2)}) %collective-permute-start.13) | collective-permute-done | bytes 917536 | tf_op jit(solution)/shard_map/ppermute | solution.py:9
  487.8 20.7 %collective-permute-done.15 = bf16[128,3584]{1,0:T(8,128)(2,1)S(1)} collective-permute-done((bf16[128,3584]{1,0:T(8,128)(2,1)S(1)}, bf16[128,3584]{1,0:T(8,128)(2,1)S(1)}, u32[]{:S(2)}, u32[]{:S(2)}) %collective-permute-start.15) | collective-permute-done | bytes 917536 | tf_op jit(solution)/shard_map/ppermute | solution.py:9
  511.0 6.2 %collective-permute-start.17 = (bf16[128,3584]{1,0:T(8,128)(2,1)S(1)}, bf16[128,3584]{1,0:T(8,128)(2,1)S(1)}, u32[]{:S(2)}, u32[]{:S(2)}) collective-permute-start(bf16[128,3584]{1,0:T(8,128)(2,1)S(1)} %fusion.5), channel_id=1, source_target_pairs={{0,7},{1,0},{2,1},{3,2},{4,3},{5,4},{6,5},{7,6},{8,15},{9,8},{10,9... | collective-permute-start | bytes 2752520 | tf_op jit(solution)/shard_map/ppermute | solution.py:9
  517.2 11.6 %collective-permute-done.17 = bf16[128,3584]{1,0:T(8,128)(2,1)S(1)} collective-permute-done((bf16[128,3584]{1,0:T(8,128)(2,1)S(1)}, bf16[128,3584]{1,0:T(8,128)(2,1)S(1)}, u32[]{:S(2)}, u32[]{:S(2)}) %collective-permute-start.17) | collective-permute-done | bytes 917536 | tf_op jit(solution)/shard_map/ppermute | solution.py:9
  530.7 15.6 %collective-permute-done.18 = bf16[128,3584]{1,0:T(8,128)(2,1)S(1)} collective-permute-done((bf16[128,3584]{1,0:T(8,128)(2,1)S(1)}, bf16[128,3584]{1,0:T(8,128)(2,1)S(1)}, u32[]{:S(2)}, u32[]{:S(2)}) %collective-permute-start.18) | collective-permute-done | bytes 917536 | tf_op jit(solution)/shard_map/ppermute | solution.py:9
  546.5 28.6 %collective-permute-done.19 = bf16[128,3584]{1,0:T(8,128)(2,1)S(1)} collective-permute-done((bf16[128,3584]{1,0:T(8,128)(2,1)S(1)}, bf16[128,3584]{1,0:T(8,128)(2,1)S(1)}, u32[]{:S(2)}, u32[]{:S(2)}) %collective-permute-start.19) | collective-permute-done | bytes 917536 | tf_op jit(solution)/shard_map/ppermute | solution.py:9
  575.2 14.9 %collective-permute-done.20 = bf16[128,3584]{1,0:T(8,128)(2,1)S(1)} collective-permute-done((bf16[128,3584]{1,0:T(8,128)(2,1)S(1)}, bf16[128,3584]{1,0:T(8,128)(2,1)S(1)}, u32[]{:S(2)}, u32[]{:S(2)}) %collective-permute-start.20) | collective-permute-done | bytes 917536 | tf_op jit(solution)/shard_map/ppermute | solution.py:9
  591.1 6.1 %convert_element_type.81 = f32[3584,512]{1,0:T(8,128)} convert(bf16[3584,512]{1,0:T(8,128)(2,1)} %reduce-scatter.2.cloned.1.call-done) | non-fusion elementwise | flops 1835008 | bytes 11010048 | tf_op jit(solution)/shard_map/convert_element_type | solution.py:57
  (92 shorter events, 112.4 us)
Async XLA Ops:
  7.2 584.0 %reduce-scatter.2.cloned.1.call-start = ((), (), s32[]{:S(2)}) async-start(), calls=%async_computation.1 | async-start | bytes 11010048 | tf_op jit(solution)/shard_map/reduce_scatter | solution.py:55
  7.2 25.6 %collective-permute-start.21 = (bf16[128,3584]{1,0:T(8,128)(2,1)}, bf16[128,3584]{1,0:T(8,128)(2,1)S(1)}, u32[]{:S(2)}, u32[]{:S(2)}) collective-permute-start(bf16[128,3584]{1,0:T(8,128)(2,1)} %param.5), channel_id=1, source_target_pairs={{0,7},{1,0},{2,1},{3,2},{4,3},{5,4},{6,5},{7,6},{8,15},{9,8},{10,9... | collective-permute-start | bytes 2752520 | tf_op jit(solution)/shard_map/ppermute | solution.py:9
  34.1 21.3 %collective-permute-start.22 = (bf16[128,3584]{1,0:T(8,128)(2,1)S(1)}, bf16[128,3584]{1,0:T(8,128)(2,1)S(1)}, u32[]{:S(2)}, u32[]{:S(2)}) collective-permute-start(bf16[128,3584]{1,0:T(8,128)(2,1)S(1)} %broadcast_select_fusion), channel_id=1, source_target_pairs={{0,6},{1,7},{2,0},{3,1},{4,2},{5,3},{6,4},{7,5},{8,14},{9,15},{10,... | collective-permute-start | bytes 2752520 | tf_op jit(solution)/shard_map/ppermute | solution.py:9
  56.4 22.1 %collective-permute-start.23 = (bf16[128,3584]{1,0:T(8,128)(2,1)}, bf16[128,3584]{1,0:T(8,128)(2,1)}, u32[]{:S(2)}, u32[]{:S(2)}) collective-permute-start(bf16[128,3584]{1,0:T(8,128)(2,1)} %broadcast_select_fusion.2), channel_id=1, source_target_pairs={{0,4},{1,5},{2,6},{3,7},{4,0},{5,1},{6,2},{7,3},{8,12},{9,13},{10,... | collective-permute-start | bytes 2752520 | tf_op jit(solution)/shard_map/ppermute | solution.py:9
  80.7 33.1 %collective-permute-start.24 = (bf16[128,3584]{1,0:T(8,128)(2,1)}, bf16[128,3584]{1,0:T(8,128)(2,1)}, u32[]{:S(2)}, u32[]{:S(2)}) collective-permute-start(bf16[128,3584]{1,0:T(8,128)(2,1)} %broadcast_select_fusion.4), channel_id=1, source_target_pairs={{0,7},{1,0},{2,1},{3,2},{4,3},{5,4},{6,5},{7,6},{8,15},{9,8},{10,9... | collective-permute-start | bytes 2752520 | tf_op jit(solution)/shard_map/ppermute | solution.py:9
  88.7 24.2 %collective-permute-start = (bf16[128,1024]{1,0:T(8,128)(2,1)}, bf16[128,1024]{1,0:T(8,128)(2,1)}, u32[]{:S(2)}, u32[]{:S(2)}) collective-permute-start(bf16[128,1024]{1,0:T(8,128)(2,1)} %multiply_convert_fusion), channel_id=1, source_target_pairs={{0,56},{8,0},{16,8},{24,16},{32,24},{40,32},{48,40},{56,48},{1,57}... | collective-permute-start | bytes 786440 | tf_op jit(solution)/shard_map/ppermute | solution.py:9
  113.8 8.2 %collective-permute-start.1 = (bf16[128,1024]{1,0:T(8,128)(2,1)}, bf16[128,1024]{1,0:T(8,128)(2,1)}, u32[]{:S(2)}, u32[]{:S(2)}) collective-permute-start(bf16[128,1024]{1,0:T(8,128)(2,1)} %broadcast_select_fusion.6), channel_id=1, source_target_pairs={{0,48},{8,56},{16,0},{24,8},{32,16},{40,24},{48,32},{56,40},{1,49}... | collective-permute-start | bytes 786440 | tf_op jit(solution)/shard_map/ppermute | solution.py:9
  113.8 42.6 %collective-permute-start.25 = (bf16[128,3584]{1,0:T(8,128)(2,1)}, bf16[128,3584]{1,0:T(8,128)(2,1)}, u32[]{:S(2)}, u32[]{:S(2)}) collective-permute-start(bf16[128,3584]{1,0:T(8,128)(2,1)} %collective-permute-done.24), channel_id=1, source_target_pairs={{0,7},{1,0},{2,1},{3,2},{4,3},{5,4},{6,5},{7,6},{8,15},{9,8},{10,9... | collective-permute-start | bytes 2752520 | tf_op jit(solution)/shard_map/ppermute | solution.py:9
  122.9 23.4 %collective-permute-start.2 = (bf16[128,1024]{1,0:T(8,128)(2,1)S(1)}, bf16[128,1024]{1,0:T(8,128)(2,1)}, u32[]{:S(2)}, u32[]{:S(2)}) collective-permute-start(bf16[128,1024]{1,0:T(8,128)(2,1)S(1)} %broadcast_select_fusion.7), channel_id=1, source_target_pairs={{0,32},{8,40},{16,48},{24,56},{32,0},{40,8},{48,16},{56,24},{1,33}... | collective-permute-start | bytes 786440 | tf_op jit(solution)/shard_map/ppermute | solution.py:9
  146.4 6.4 %collective-permute-start.4 = (bf16[128,1024]{1,0:T(8,128)(2,1)S(1)}, bf16[128,1024]{1,0:T(8,128)(2,1)S(1)}, u32[]{:S(2)}, u32[]{:S(2)}) collective-permute-start(bf16[128,1024]{1,0:T(8,128)(2,1)S(1)} %broadcast_select_fusion.8), channel_id=1, source_target_pairs={{0,56},{8,0},{16,8},{24,16},{32,24},{40,32},{48,40},{56,48},{1,57}... | collective-permute-start | bytes 786440 | tf_op jit(solution)/shard_map/ppermute | solution.py:9
  152.8 10.9 %collective-permute-start.6 = (bf16[128,1024]{1,0:T(8,128)(2,1)S(1)}, bf16[128,1024]{1,0:T(8,128)(2,1)S(1)}, u32[]{:S(2)}, u32[]{:S(2)}) collective-permute-start(bf16[128,1024]{1,0:T(8,128)(2,1)S(1)} %collective-permute-done.4), channel_id=1, source_target_pairs={{0,56},{8,0},{16,8},{24,16},{32,24},{40,32},{48,40},{56,48},{1,57}... | collective-permute-start | bytes 786440 | tf_op jit(solution)/shard_map/ppermute | solution.py:9
  156.4 73.5 %collective-permute-start.26 = (bf16[128,3584]{1,0:T(8,128)(2,1)}, bf16[128,3584]{1,0:T(8,128)(2,1)S(1)}, u32[]{:S(2)}, u32[]{:S(2)}) collective-permute-start(bf16[128,3584]{1,0:T(8,128)(2,1)} %collective-permute-done.25), channel_id=1, source_target_pairs={{0,7},{1,0},{2,1},{3,2},{4,3},{5,4},{6,5},{7,6},{8,15},{9,8},{10,9... | collective-permute-start | bytes 2752520 | tf_op jit(solution)/shard_map/ppermute | solution.py:9
  162.0 67.9 %collective-permute-start.3 = (bf16[128,3584]{1,0:T(8,128)(2,1)S(1)}, bf16[128,3584]{1,0:T(8,128)(2,1)S(1)}, u32[]{:S(2)}, u32[]{:S(2)}) collective-permute-start(bf16[128,3584]{1,0:T(8,128)(2,1)S(1)} %convolution_convert_fusion), channel_id=1, source_target_pairs={{0,7},{1,0},{2,1},{3,2},{4,3},{5,4},{6,5},{7,6},{8,15},{9,8},{10,9... | collective-permute-start | bytes 2752520 | tf_op jit(solution)/shard_map/ppermute | solution.py:9
  163.7 39.8 %collective-permute-start.8 = (bf16[128,1024]{1,0:T(8,128)(2,1)S(1)}, bf16[128,1024]{1,0:T(8,128)(2,1)S(1)}, u32[]{:S(2)}, u32[]{:S(2)}) collective-permute-start(bf16[128,1024]{1,0:T(8,128)(2,1)S(1)} %collective-permute-done.6), channel_id=1, source_target_pairs={{0,56},{8,0},{16,8},{24,16},{32,24},{40,32},{48,40},{56,48},{1,57}... | collective-permute-start | bytes 786440 | tf_op jit(solution)/shard_map/ppermute | solution.py:9
  203.5 10.4 %collective-permute-start.10 = (bf16[128,1024]{1,0:T(8,128)(2,1)S(1)}, bf16[128,1024]{1,0:T(8,128)(2,1)S(1)}, u32[]{:S(2)}, u32[]{:S(2)}) collective-permute-start(bf16[128,1024]{1,0:T(8,128)(2,1)S(1)} %collective-permute-done.8), channel_id=1, source_target_pairs={{0,56},{8,0},{16,8},{24,16},{32,24},{40,32},{48,40},{56,48},{1,57}... | collective-permute-start | bytes 786440 | tf_op jit(solution)/shard_map/ppermute | solution.py:9
  213.9 11.4 %collective-permute-start.12 = (bf16[128,1024]{1,0:T(8,128)(2,1)S(1)}, bf16[128,1024]{1,0:T(8,128)(2,1)S(1)}, u32[]{:S(2)}, u32[]{:S(2)}) collective-permute-start(bf16[128,1024]{1,0:T(8,128)(2,1)S(1)} %collective-permute-done.10), channel_id=1, source_target_pairs={{0,56},{8,0},{16,8},{24,16},{32,24},{40,32},{48,40},{56,48},{1,57}... | collective-permute-start | bytes 786440 | tf_op jit(solution)/shard_map/ppermute | solution.py:9
  225.3 11.4 %collective-permute-start.14 = (bf16[128,1024]{1,0:T(8,128)(2,1)S(1)}, bf16[128,1024]{1,0:T(8,128)(2,1)S(1)}, u32[]{:S(2)}, u32[]{:S(2)}) collective-permute-start(bf16[128,1024]{1,0:T(8,128)(2,1)S(1)} %collective-permute-done.12), channel_id=1, source_target_pairs={{0,56},{8,0},{16,8},{24,16},{32,24},{40,32},{48,40},{56,48},{1,57}... | collective-permute-start | bytes 786440 | tf_op jit(solution)/shard_map/ppermute | solution.py:9
  229.9 26.4 %collective-permute-start.27 = (bf16[128,3584]{1,0:T(8,128)(2,1)S(1)}, bf16[128,3584]{1,0:T(8,128)(2,1)S(1)}, u32[]{:S(2)}, u32[]{:S(2)}) collective-permute-start(bf16[128,3584]{1,0:T(8,128)(2,1)S(1)} %collective-permute-done.26), channel_id=1, source_target_pairs={{0,7},{1,0},{2,1},{3,2},{4,3},{5,4},{6,5},{7,6},{8,15},{9,8},{10,9... | collective-permute-start | bytes 2752520 | tf_op jit(solution)/shard_map/ppermute | solution.py:9
  233.4 139.9 %collective-permute-start.5 = (bf16[128,3584]{1,0:T(8,128)(2,1)}, bf16[128,3584]{1,0:T(8,128)(2,1)}, u32[]{:S(2)}, u32[]{:S(2)}) collective-permute-start(bf16[128,3584]{1,0:T(8,128)(2,1)} %add_convert_fusion.1), channel_id=1, source_target_pairs={{0,7},{1,0},{2,1},{3,2},{4,3},{5,4},{6,5},{7,6},{8,15},{9,8},{10,9... | collective-permute-start | bytes 2752520 | tf_op jit(solution)/shard_map/ppermute | solution.py:9
  236.6 101.4 %collective-permute-start.16 = (bf16[128,1024]{1,0:T(8,128)(2,1)S(1)}, bf16[128,1024]{1,0:T(8,128)(2,1)S(1)}, u32[]{:S(2)}, u32[]{:S(2)}) collective-permute-start(bf16[128,1024]{1,0:T(8,128)(2,1)S(1)} %collective-permute-done.14), channel_id=1, source_target_pairs={{0,56},{8,0},{16,8},{24,16},{32,24},{40,32},{48,40},{56,48},{1,57}... | collective-permute-start | bytes 786440 | tf_op jit(solution)/shard_map/ppermute | solution.py:9
  256.3 39.9 %collective-permute-start.28 = (bf16[128,3584]{1,0:T(8,128)(2,1)S(1)}, bf16[128,3584]{1,0:T(8,128)(2,1)S(1)}, u32[]{:S(2)}, u32[]{:S(2)}) collective-permute-start(bf16[128,3584]{1,0:T(8,128)(2,1)S(1)} %collective-permute-done.27), channel_id=1, source_target_pairs={{0,7},{1,0},{2,1},{3,2},{4,3},{5,4},{6,5},{7,6},{8,15},{9,8},{10,9... | collective-permute-start | bytes 2752520 | tf_op jit(solution)/shard_map/ppermute | solution.py:9
  296.2 21.1 %collective-permute-start.29 = (bf16[128,3584]{1,0:T(8,128)(2,1)S(1)}, bf16[128,3584]{1,0:T(8,128)(2,1)S(1)}, u32[]{:S(2)}, u32[]{:S(2)}) collective-permute-start(bf16[128,3584]{1,0:T(8,128)(2,1)S(1)} %collective-permute-done.28), channel_id=1, source_target_pairs={{0,7},{1,0},{2,1},{3,2},{4,3},{5,4},{6,5},{7,6},{8,15},{9,8},{10,9... | collective-permute-start | bytes 2752520 | tf_op jit(solution)/shard_map/ppermute | solution.py:9
  317.3 20.8 %collective-permute-start.30 = (bf16[128,3584]{1,0:T(8,128)(2,1)S(1)}, bf16[128,3584]{1,0:T(8,128)(2,1)S(1)}, u32[]{:S(2)}, u32[]{:S(2)}) collective-permute-start(bf16[128,3584]{1,0:T(8,128)(2,1)S(1)} %collective-permute-done.29), channel_id=1, source_target_pairs={{0,7},{1,0},{2,1},{3,2},{4,3},{5,4},{6,5},{7,6},{8,15},{9,8},{10,9... | collective-permute-start | bytes 2752520 | tf_op jit(solution)/shard_map/ppermute | solution.py:9
  379.4 23.3 %collective-permute-start.7 = (bf16[128,3584]{1,0:T(8,128)(2,1)S(1)}, bf16[128,3584]{1,0:T(8,128)(2,1)S(1)}, u32[]{:S(2)}, u32[]{:S(2)}) collective-permute-start(bf16[128,3584]{1,0:T(8,128)(2,1)S(1)} %fusion), channel_id=1, source_target_pairs={{0,7},{1,0},{2,1},{3,2},{4,3},{5,4},{6,5},{7,6},{8,15},{9,8},{10,9... | collective-permute-start | bytes 2752520 | tf_op jit(solution)/shard_map/ppermute | solution.py:9
  405.2 24.3 %collective-permute-start.9 = (bf16[128,3584]{1,0:T(8,128)(2,1)S(1)}, bf16[128,3584]{1,0:T(8,128)(2,1)S(1)}, u32[]{:S(2)}, u32[]{:S(2)}) collective-permute-start(bf16[128,3584]{1,0:T(8,128)(2,1)S(1)} %fusion.1), channel_id=1, source_target_pairs={{0,7},{1,0},{2,1},{3,2},{4,3},{5,4},{6,5},{7,6},{8,15},{9,8},{10,9... | collective-permute-start | bytes 2752520 | tf_op jit(solution)/shard_map/ppermute | solution.py:9
  432.1 24.1 %collective-permute-start.11 = (bf16[128,3584]{1,0:T(8,128)(2,1)S(1)}, bf16[128,3584]{1,0:T(8,128)(2,1)S(1)}, u32[]{:S(2)}, u32[]{:S(2)}) collective-permute-start(bf16[128,3584]{1,0:T(8,128)(2,1)S(1)} %fusion.2), channel_id=1, source_target_pairs={{0,7},{1,0},{2,1},{3,2},{4,3},{5,4},{6,5},{7,6},{8,15},{9,8},{10,9... | collective-permute-start | bytes 2752520 | tf_op jit(solution)/shard_map/ppermute | solution.py:9
  458.8 23.1 %collective-permute-start.13 = (bf16[128,3584]{1,0:T(8,128)(2,1)S(1)}, bf16[128,3584]{1,0:T(8,128)(2,1)S(1)}, u32[]{:S(2)}, u32[]{:S(2)}) collective-permute-start(bf16[128,3584]{1,0:T(8,128)(2,1)S(1)} %fusion.3), channel_id=1, source_target_pairs={{0,7},{1,0},{2,1},{3,2},{4,3},{5,4},{6,5},{7,6},{8,15},{9,8},{10,9... | collective-permute-start | bytes 2752520 | tf_op jit(solution)/shard_map/ppermute | solution.py:9
  484.4 24.1 %collective-permute-start.15 = (bf16[128,3584]{1,0:T(8,128)(2,1)S(1)}, bf16[128,3584]{1,0:T(8,128)(2,1)S(1)}, u32[]{:S(2)}, u32[]{:S(2)}) collective-permute-start(bf16[128,3584]{1,0:T(8,128)(2,1)S(1)} %fusion.4), channel_id=1, source_target_pairs={{0,7},{1,0},{2,1},{3,2},{4,3},{5,4},{6,5},{7,6},{8,15},{9,8},{10,9... | collective-permute-start | bytes 2752520 | tf_op jit(solution)/shard_map/ppermute | solution.py:9
  511.0 17.8 %collective-permute-start.17 = (bf16[128,3584]{1,0:T(8,128)(2,1)S(1)}, bf16[128,3584]{1,0:T(8,128)(2,1)S(1)}, u32[]{:S(2)}, u32[]{:S(2)}) collective-permute-start(bf16[128,3584]{1,0:T(8,128)(2,1)S(1)} %fusion.5), channel_id=1, source_target_pairs={{0,7},{1,0},{2,1},{3,2},{4,3},{5,4},{6,5},{7,6},{8,15},{9,8},{10,9... | collective-permute-start | bytes 2752520 | tf_op jit(solution)/shard_map/ppermute | solution.py:9
  528.8 17.5 %collective-permute-start.18 = (bf16[128,3584]{1,0:T(8,128)(2,1)S(1)}, bf16[128,3584]{1,0:T(8,128)(2,1)S(1)}, u32[]{:S(2)}, u32[]{:S(2)}) collective-permute-start(bf16[128,3584]{1,0:T(8,128)(2,1)S(1)} %collective-permute-done.17), channel_id=1, source_target_pairs={{0,1},{1,2},{2,3},{3,4},{4,5},{5,6},{6,7},{7,0},{8,9},{9,10},{10,1... | collective-permute-start | bytes 2752520 | tf_op jit(solution)/shard_map/ppermute | solution.py:9
  546.4 28.6 %collective-permute-start.19 = (bf16[128,3584]{1,0:T(8,128)(2,1)S(1)}, bf16[128,3584]{1,0:T(8,128)(2,1)S(1)}, u32[]{:S(2)}, u32[]{:S(2)}) collective-permute-start(bf16[128,3584]{1,0:T(8,128)(2,1)S(1)} %broadcast_select_fusion.1), channel_id=1, source_target_pairs={{0,2},{1,3},{2,4},{3,5},{4,6},{5,7},{6,0},{7,1},{8,10},{9,11},{10,... | collective-permute-start | bytes 2752520 | tf_op jit(solution)/shard_map/ppermute | solution.py:9
  575.1 15.0 %collective-permute-start.20 = (bf16[128,3584]{1,0:T(8,128)(2,1)S(1)}, bf16[128,3584]{1,0:T(8,128)(2,1)S(1)}, u32[]{:S(2)}, u32[]{:S(2)}) collective-permute-start(bf16[128,3584]{1,0:T(8,128)(2,1)S(1)} %broadcast_select_fusion.3), channel_id=1, source_target_pairs={{0,4},{1,5},{2,6},{3,7},{4,0},{5,1},{6,2},{7,3},{8,12},{9,13},{10,... | collective-permute-start | bytes 2752520 | tf_op jit(solution)/shard_map/ppermute | solution.py:9
  (14 other events, 1068.4 us)
Sparse Core Ops, SparseCore 0:
  373.4 14.8 reduce-scatter.1
where the time goes:
time: 613 us; the launch traced here: 604 us
  waiting for transfers between devices  371 us (61%)
  matrix products  117 us (19%)
  starting transfers between devices  85.7 us (14%)
  other arithmetic  15.9 us (3%)
  between operations  14.5 us (2%)
    ppermute x31, waiting for transfers between devices, shifted_2(): lax.ppermute(array, axis, [(i, (i + by) % devices) for i in range(devices)])  371 us
    dot_general x8, matrix products, body(): lax.dot_general(moving_hidden, moving_cotan, (((0,), (0,)), ((), ())), pr...  89.6 us
    ppermute x31, starting transfers between devices, shifted_2(): lax.ppermute(array, axis, [(i, (i + by) % devices) for i in range(devices)])  85.6 us
    dot_general x8, matrix products, body(): lax.dot_general(moving_cotan, weight, (((1,), (1,)), ((), ())), preferred...  27.8 us
  transfers between devices with their start and end apart: 32, of which 23 were waited for; matrix products, arithmetic and copies ran while one was open for 20% of the time, Pallas kernels for 0%

commit v1 on v0

v1 whole, which is shorter than its diff:
```python
import jax
import jax.numpy as jnp
from jax import lax
from jax.experimental import pallas as pl
from jax.experimental.pallas import tpu as pltpu
from jax.sharding import PartitionSpec as P

MESH = pl.DeviceIdType.MESH
BF16 = jnp.bfloat16
F32 = jnp.float32

TOK = 128
FF = 3584
D = 1024
A = 2048
B = FF - A
AH = A // 2
BH = B // 2
TILE = 512
GT = 256
NG = FF // GT
MESSAGES = 64


def column(row_vector, n):
    on_diagonal = lax.broadcasted_iota(jnp.int32, (n, n), 0) == lax.broadcasted_iota(jnp.int32, (n, n), 1)
    return jnp.sum(jnp.where(on_diagonal, jnp.broadcast_to(row_vector, (n, n)), 0.0), axis=1, keepdims=True)


def kernel(
    h_ref, c_ref, lang_ref, counts_ref, w_ref,
    gh_ref, own_ref, other_ref,
    wv, ha, hb, call, pa, pb, ra2, ra1, rax, rbx, rb2, rb1, gst,
    ss, rs, gss, grs, gls, ls,
):
    dp, row, col = lax.axis_index("dp"), lax.axis_index("row"), lax.axis_index("col")
    xl, y = row // 4, row % 4
    z, h = col // 2, col % 2
    q = 1 - h
    zp, zm, zo = (z + 1) % 4, (z + 3) % 4, (z + 2) % 4
    yp, ym, yo = (y + 1) % 4, (y + 3) % 4, (y + 2) % 4
    to_zp, to_zm = (dp, row, zp * 2 + h), (dp, row, zm * 2 + h)
    to_x2 = (dp, row, z * 2 + q)
    to_yp, to_ym = (dp, xl * 4 + yp, col), (dp, xl * 4 + ym, col)
    to_xl = (dp, (1 - xl) * 4 + y, col)
    to_dp = (1 - dp, row, col)
    neighbours = (to_zp, to_zm, to_x2, to_yp, to_ym, to_xl, to_dp)

    barrier = pltpu.get_barrier_semaphore()
    for device in neighbours:
        pl.semaphore_signal(barrier, inc=1, device_id=device, device_id_type=MESH)

    load_w = pltpu.make_async_copy(w_ref, wv, ls.at[0])
    load_a = pltpu.make_async_copy(h_ref.at[:, pl.ds(0, A)], ha.at[col], ls.at[1])
    load_b = pltpu.make_async_copy(h_ref.at[:, pl.ds(A, B)], hb.at[col], ls.at[2])
    load_w.start()
    load_a.start()
    load_b.start()

    lang_weight = column(jnp.sqrt(512.0 / counts_ref[...].astype(F32)), 32)
    matches = lang_ref[...] == lax.broadcasted_iota(jnp.int32, (32, TOK), 0)
    weight_row = jnp.sum(jnp.where(matches, lang_weight, 0.0), axis=0, keepdims=True)
    token_weight = column(weight_row, TOK)
    call[row] = (c_ref[...].astype(F32) * token_weight).astype(BF16)

    pl.semaphore_wait(barrier, len(neighbours))

    sent = []

    def send(src, dst, device):
        i = len(sent)
        copy = pltpu.make_async_remote_copy(
            src_ref=src, dst_ref=dst, send_sem=ss.at[i], recv_sem=rs.at[i], device_id=device, device_id_type=MESH
        )
        copy.start()
        sent.append(copy)
        return copy

    def got(*copies):
        for copy in copies:
            copy.wait_recv()

    def pass_on(ref, block, device, lo=None, n=None):
        at = ref.at[block] if lo is None else ref.at[block, :, pl.ds(lo, n)]
        return send(at, at, device)

    h_a, h_b = h_ref.at[:, pl.ds(0, A)], h_ref.at[:, pl.ds(A, B)]
    own_b = [send(h_b, hb.at[col], d) for d in (to_zp, to_zm)]
    own_ax = send(h_a, ha.at[col], to_x2)
    own_cx = pass_on(call, row, to_xl)
    own_cy = [pass_on(call, row, d) for d in (to_yp, to_ym)]
    own_a = [send(h_a, ha.at[col], d) for d in (to_zp, to_zm)]

    def cblock(yy, partner):
        return ((1 - xl) if partner else xl) * 4 + yy

    def chalf(block, half, device):
        at = call.at[block, pl.ds(half * 64, 64), :]
        return send(at, at, device)

    got(own_cx)
    par_cy = [pass_on(call, cblock(y, True), d) for d in (to_yp, to_ym)]
    got(*own_cy)
    own_c2 = [chalf(cblock(ym, False), 0, to_yp), chalf(cblock(yp, False), 1, to_ym)]

    got(*own_b)
    fwd_b = [pass_on(hb, zm * 2 + h, to_zp, 0, BH), pass_on(hb, zp * 2 + h, to_zm, BH, BH)]
    x_b = [pass_on(hb, zm * 2 + h, to_x2), pass_on(hb, zp * 2 + h, to_x2), send(h_b, hb.at[col], to_x2)]

    got(own_ax)
    par_a = [pass_on(ha, z * 2 + q, d) for d in (to_zp, to_zm)]
    got(*par_cy)
    par_c2 = [chalf(cblock(ym, True), 0, to_yp), chalf(cblock(yp, True), 1, to_ym)]
    got(*own_a)
    fwd_a = [pass_on(ha, zm * 2 + h, to_zp, 0, AH), pass_on(ha, zp * 2 + h, to_zm, AH, AH)]
    got(*own_c2, *par_c2)
    load_w.wait()

    def partial_sums(at, zd):
        cots = call[pl.ds(zd * 2, 2)].reshape(2 * TOK, D)

        def tile(ref, base):
            def step(j, carry):
                rows = pl.ds(pl.multiple_of(base + j * TILE, TILE), TILE)
                part = lax.dot_general(cots, wv[rows, :], (((1,), (1,)), ((), ())), preferred_element_type=F32)
                part = part.astype(BF16).reshape(2, TOK, TILE)
                ref[at, :, :, pl.ds(pl.multiple_of(j * TILE, TILE), TILE)] = part
                return carry
            return step

        lax.fori_loop(0, A // TILE, tile(pa, 0), 0)
        lax.fori_loop(0, B // TILE, tile(pb, A), 0)

    partial_sums(0, zo)
    got(*fwd_b)
    x_b2 = [pass_on(hb, zo * 2 + h, to_x2, 0, BH), pass_on(hb, zo * 2 + h, to_x2, BH, BH)]
    partial_sums(1, zp)
    partial_sums(2, zm)
    got(*par_a)
    fwd_pa = [pass_on(ha, zm * 2 + q, to_zp, 0, AH), pass_on(ha, zp * 2 + q, to_zm, AH, AH)]
    partial_sums(3, z)

    def far_a(hh):
        return [
            send(pa.at[0, hh, :, pl.ds(0, AH)], ra2.at[hh, 0], to_zp),
            send(pa.at[0, hh, :, pl.ds(AH, AH)], ra2.at[hh, 1], to_zm),
        ]

    far_pa = far_a(q)
    cross_b = [send(pb.at[k, q], rbx.at[k], to_x2) for k in range(4)]
    far_oa = far_a(h)

    load_a.wait()
    load_b.wait()
    got(*fwd_a, *fwd_pa)

    def weight_tiles(ref, base, lo, hi):
        def step(j, carry):
            cols = pl.ds(pl.multiple_of(j * GT, GT), GT)
            hid = ref[:, :, cols].reshape(8 * TOK, GT)
            tile = base + j
            for half in range(2):
                cots = call[:, :, pl.ds(half * 512, 512)].reshape(8 * TOK, 512)
                out = lax.dot_general(hid, cots, (((0,), (0,)), ((), ())), preferred_element_type=F32)
                gst[tile, half] = out.astype(BF16)
            weight_copy(tile).start()
            weight_send(tile).start()
            return carry
        lax.fori_loop(lo, hi, step, 0)

    def weight_copy(tile):
        rows = pl.ds(pl.multiple_of(tile * GT, GT), GT)
        return pltpu.make_async_copy(gst.at[tile, dp], own_ref.at[rows, :], gls.at[tile])

    def weight_send(tile):
        rows = pl.ds(pl.multiple_of(tile * GT, GT), GT)
        return pltpu.make_async_remote_copy(
            src_ref=gst.at[tile, 1 - dp], dst_ref=other_ref.at[rows, :], send_sem=gss.at[tile],
            recv_sem=grs.at[tile], device_id=to_dp, device_id_type=MESH,
        )

    def add(ref, at, *others):
        total = ref[at].astype(F32)
        for other, other_at in others:
            total = total + other[other_at].astype(F32)
        ref[at] = total.astype(BF16)

    everything = slice(None)

    def near_a(hh):
        add(pa, (1, hh, everything, slice(0, AH)), (ra2, (hh, 0)))
        add(pa, (2, hh, everything, slice(AH, A)), (ra2, (hh, 1)))
        return [send(pa.at[1, hh], ra1.at[hh, 0], to_zp), send(pa.at[2, hh], ra1.at[hh, 1], to_zm)]

    weight_tiles(ha, 0, 0, 4)
    got(*far_pa)
    near_pa = near_a(q)
    got(cross_b[0])
    add(pb, (0, h), (rbx, 0))
    far_b = [
        send(pb.at[0, h, :, pl.ds(0, BH)], rb2.at[0], to_zp),
        send(pb.at[0, h, :, pl.ds(BH, BH)], rb2.at[1], to_zm),
    ]
    got(*far_oa)
    near_oa = near_a(h)
    weight_tiles(ha, 0, 4, A // GT)
    got(*x_b, *x_b2)
    weight_tiles(hb, A // GT, 0, 2)
    got(*near_pa)
    add(pa, (3, q), (ra1, (q, 0)), (ra1, (q, 1)))
    last_ax = send(pa.at[3, q], rax, to_x2)
    got(cross_b[1], cross_b[2], *far_b)
    add(pb, (1, h), (rbx, 1))
    add(pb, (1, h, everything, slice(0, BH)), (rb2, 0))
    add(pb, (2, h), (rbx, 2))
    add(pb, (2, h, everything, slice(BH, B)), (rb2, 1))
    near_b = [send(pb.at[1, h], rb1.at[0], to_zp), send(pb.at[2, h], rb1.at[1], to_zm)]
    weight_tiles(hb, A // GT, 2, B // GT)
    got(cross_b[3])
    add(pb, (3, h), (rbx, 3))
    got(*near_oa)
    add(pa, (3, h), (ra1, (h, 0)), (ra1, (h, 1)))
    got(last_ax)
    add(pa, (3, h), (rax, everything))
    out_a = pltpu.make_async_copy(pa.at[3, h], gh_ref.at[:, pl.ds(0, A)], ls.at[3])
    out_a.start()
    got(*near_b)
    add(pb, (3, h), (rb1, 0), (rb1, 1))
    out_b = pltpu.make_async_copy(pb.at[3, h], gh_ref.at[:, pl.ds(A, B)], ls.at[4])
    out_b.start()

    for copy in sent:
        copy.wait_send()

    def finish(tile, carry):
        weight_copy(tile).wait()
        weight_send(tile).wait()
        return carry

    lax.fori_loop(0, NG, finish, 0)
    out_a.wait()
    out_b.wait()


def body(hidden, cotangent, language, counts, weight):
    anywhere = pl.BlockSpec(memory_space=pl.ANY)
    vmem = pl.BlockSpec(memory_space=pltpu.VMEM)
    dma = pltpu.SemaphoreType.DMA
    grad_hidden, own, other = pl.pallas_call(
        kernel,
        out_shape=(
            jax.ShapeDtypeStruct((TOK, FF), BF16),
            jax.ShapeDtypeStruct((FF, D // 2), BF16),
            jax.ShapeDtypeStruct((FF, D // 2), BF16),
        ),
        in_specs=[anywhere, vmem, vmem, vmem, anywhere],
        out_specs=(anywhere, anywhere, anywhere),
        scratch_shapes=[
            pltpu.VMEM((FF, D), BF16),
            pltpu.VMEM((8, TOK, A), BF16),
            pltpu.VMEM((8, TOK, B), BF16),
            pltpu.VMEM((8, TOK, D), BF16),
            pltpu.VMEM((4, 2, TOK, A), BF16),
            pltpu.VMEM((4, 2, TOK, B), BF16),
            pltpu.VMEM((2, 2, TOK, AH), BF16),
            pltpu.VMEM((2, 2, TOK, A), BF16),
            pltpu.VMEM((TOK, A), BF16),
            pltpu.VMEM((4, TOK, B), BF16),
            pltpu.VMEM((2, TOK, BH), BF16),
            pltpu.VMEM((2, TOK, B), BF16),
            pltpu.VMEM((NG, 2, GT, D // 2), BF16),
            dma((MESSAGES,)),
            dma((MESSAGES,)),
            dma((NG,)),
            dma((NG,)),
            dma((NG,)),
            dma((5,)),
        ],
        compiler_params=pltpu.CompilerParams(
            collective_id=0, has_side_effects=True, vmem_limit_bytes=56 * 2**20
        ),
        cost_estimate=pl.CostEstimate(flops=4 * 1024 * FF * D, bytes_accessed=24 * 2**20, transcendentals=32),
    )(hidden, cotangent, language.reshape(1, TOK), counts.reshape(1, 32), weight)
    return grad_hidden, own.astype(F32) + other.astype(F32)


def solution(mesh):
    placed = (
        P(("dp", "col"), "row"),
        P(("dp", "row"), "col"),
        P(("dp", "row")),
        P(),
        P("row", "col"),
    )
    return jax.shard_map(
        body,
        mesh=mesh,
        in_specs=placed,
        out_specs=(P(("dp", "col"), "row"), P("row", ("col", "dp"))),
        check_vma=False,
    )
```

time: 613 us -> 117 us (0.19); the launches traced: 604 us -> 116 us
  waiting for transfers between devices: 371 us -> 0 us
  matrix products: 117 us -> 0 us
  Pallas kernels: 0 us -> 107 us
  starting transfers between devices: 85.7 us -> 0 us
  between operations: 14.5 us -> 0.65 us
  other arithmetic: 15.9 us -> 7.39 us
    ppermute x31 -> x0, waiting for transfers between devices: 371 us -> none  [shifted_2(): lax.ppermute(array, axis, [(i, (i + by) % devices) for i in range(devices)])]
    dot_general x16 -> x0, matrix products: 117 us -> none  [the longest x8 89.6 us: body(): lax.dot_general(moving_hidden, moving_cotan, (((0,), (0,)), ((), ())), pr...]
    pallas_call x0 -> x1, Pallas kernels: none -> 107 us  [body(): pl.pallas_call(kernel, out_shape=(jax.ShapeDtypeStruct((TOK, FF), BF16),...]
    ppermute x31 -> x0, starting transfers between devices: 85.6 us -> none  [shifted_2(): lax.ppermute(array, axis, [(i, (i + by) % devices) for i in range(devices)])]
    select_n x9 -> x0, other arithmetic: 7.57 us -> none  [the longest x3 4.5 us: body(): jnp.where(row_at >> bit_pos & 1 == 1, shifted, moving_hidden)]
    add x0 -> x1, other arithmetic: none -> 7.39 us  [body(): return (grad_hidden, own.astype(F32) + other.astype(F32))]
    convert_element_type x2 -> x0, other arithmetic: 6.95 us -> none  [the longest x1 6.14 us: body(): grad_weight = lax.psum_scatter(weight_grad.astype(jnp.bfloat16), 'dp', sc...]
  transfers between devices with their start and end apart: 32 -> 0, of which waited for: 23 -> 0; matrix products, arithmetic and copies ran while one was open for 20% -> 0% of each run, Pallas kernels for 0% -> 0%
where the time goes in v1:
time: 117 us; the launch traced here: 116 us
  Pallas kernels  107 us (91%)
  other arithmetic  7.39 us (6%)
    pallas_call x1, Pallas kernels, body(): pl.pallas_call(kernel, out_shape=(jax.ShapeDtypeStruct((TOK, FF), BF16),...  107 us
    add x1, other arithmetic, body(): return (grad_hidden, own.astype(F32) + other.astype(F32))  7.39 us

profile of v1, /device:TPU:2, one launch (start us, length us, event | category | flops | bytes accessed | tf_op | source)
XLA Modules:
  0.0 115.5 jit_solution(14913993069699699096)
XLA Ops:
  0.6 106.6 %shard_map.68 = (bf16[128,3584]{1,0:T(8,128)(2,1)}, bf16[3584,512]{1,0:T(8,128)(2,1)}, bf16[3584,512]{1,0:T(8,128)(2,1)}) custom-call(bf16[128,3584]{1,0:T(8,128)(2,1)} %h_ref.1, bf16[128,1024]{1,0:T(8,128)(2,1)} %c_ref.1, s32[1,128]{1,0:T(1,128)} %bitcast.2, s32[1,32]{1,0:T(1,128)} %bitcast.3, bf16[3584,1024]{1,0:T(8,128)(2,1)} %w_ref.1), custom_call_target="tpu_custom_call" | custom-call | flops 15032385536 | bytes 25165824 | tf_op jit(solution)/shard_map/pallas_call | solution.py:249
  107.2 0.0 copy-start
  107.2 7.4 %convert_add_fusion = f32[3584,512]{1,0:T(8,128)} fusion(bf16[3584,512]{1,0:T(8,128)(2,1)} %get-tuple-element.7, bf16[3584,512]{1,0:T(8,128)(2,1)} %get-tuple-element.6), kind=kLoop, calls=%fused_computation | loop fusion | flops 5505024 | bytes 14680064 | tf_op jit(solution)/shard_map/add | solution.py:284
  114.6 0.0 copy-done
  114.6 0.9 copy.8
Async XLA Ops:
  107.2 7.4 %copy-start = (bf16[128,3584]{1,0:T(8,128)(2,1)S(1)}, bf16[128,3584]{1,0:T(8,128)(2,1)}, u32[]{:S(2)}) copy-start(bf16[128,3584]{1,0:T(8,128)(2,1)} %get-tuple-element.10) | copy-start | bytes 2752516

commit v2 on v1

--- a/solution.py
+++ b/solution.py
@@ -29,9 +29,9 @@
 
 def kernel(
     h_ref, c_ref, lang_ref, counts_ref, w_ref,
-    gh_ref, own_ref, other_ref,
-    wv, ha, hb, call, pa, pb, ra2, ra1, rax, rbx, rb2, rb1, gst,
-    ss, rs, gss, grs, gls, ls,
+    gh_ref, gw_ref,
+    wv, ha, hb, call, pa, pb, ra2, ra1, rax, rbx, rb2, rb1, gst, grv,
+    ss, rs, gss, grs, ls,
 ):
     dp, row, col = lax.axis_index("dp"), lax.axis_index("row"), lax.axis_index("col")
     xl, y = row // 4, row % 4
@@ -159,25 +159,31 @@
             cols = pl.ds(pl.multiple_of(j * GT, GT), GT)
             hid = ref[:, :, cols].reshape(8 * TOK, GT)
             tile = base + j
-            for half in range(2):
-                cots = call[:, :, pl.ds(half * 512, 512)].reshape(8 * TOK, 512)
+
+            def product(part):
+                cots = call[:, :, pl.ds(pl.multiple_of(part * 512, 512), 512)].reshape(8 * TOK, 512)
                 out = lax.dot_general(hid, cots, (((0,), (0,)), ((), ())), preferred_element_type=F32)
-                gst[tile, half] = out.astype(BF16)
-            weight_copy(tile).start()
+                return out.astype(BF16)
+
+            gst[tile] = product(1 - dp)
             weight_send(tile).start()
+            gw_ref[weight_rows(tile), :] = product(dp).astype(F32)
             return carry
         lax.fori_loop(lo, hi, step, 0)
 
-    def weight_copy(tile):
-        rows = pl.ds(pl.multiple_of(tile * GT, GT), GT)
-        return pltpu.make_async_copy(gst.at[tile, dp], own_ref.at[rows, :], gls.at[tile])
+    def weight_rows(tile):
+        return pl.ds(pl.multiple_of(tile * GT, GT), GT)
 
     def weight_send(tile):
-        rows = pl.ds(pl.multiple_of(tile * GT, GT), GT)
         return pltpu.make_async_remote_copy(
-            src_ref=gst.at[tile, 1 - dp], dst_ref=other_ref.at[rows, :], send_sem=gss.at[tile],
+            src_ref=gst.at[tile], dst_ref=grv.at[tile], send_sem=gss.at[tile],
             recv_sem=grs.at[tile], device_id=to_dp, device_id_type=MESH,
         )
+
+    def weight_sum(tile, carry):
+        weight_send(tile).wait()
+        gw_ref[weight_rows(tile), :] += grv[tile].astype(F32)
+        return carry
 
     def add(ref, at, *others):
         total = ref[at].astype(F32)
@@ -216,45 +222,31 @@
     add(pb, (2, h, everything, slice(BH, B)), (rb2, 1))
     near_b = [send(pb.at[1, h], rb1.at[0], to_zp), send(pb.at[2, h], rb1.at[1], to_zm)]
     weight_tiles(hb, A // GT, 2, B // GT)
+    lax.fori_loop(0, NG, weight_sum, 0)
     got(cross_b[3])
     add(pb, (3, h), (rbx, 3))
     got(*near_oa)
     add(pa, (3, h), (ra1, (h, 0)), (ra1, (h, 1)))
     got(last_ax)
     add(pa, (3, h), (rax, everything))
-    out_a = pltpu.make_async_copy(pa.at[3, h], gh_ref.at[:, pl.ds(0, A)], ls.at[3])
-    out_a.start()
+    gh_ref[:, 0:A] = pa[3, h]
     got(*near_b)
     add(pb, (3, h), (rb1, 0), (rb1, 1))
-    out_b = pltpu.make_async_copy(pb.at[3, h], gh_ref.at[:, pl.ds(A, B)], ls.at[4])
-    out_b.start()
+    gh_ref[:, A:FF] = pb[3, h]
 
     for copy in sent:
         copy.wait_send()
-
-    def finish(tile, carry):
-        weight_copy(tile).wait()
-        weight_send(tile).wait()
-        return carry
-
-    lax.fori_loop(0, NG, finish, 0)
-    out_a.wait()
-    out_b.wait()
 
 
 def body(hidden, cotangent, language, counts, weight):
     anywhere = pl.BlockSpec(memory_space=pl.ANY)
     vmem = pl.BlockSpec(memory_space=pltpu.VMEM)
     dma = pltpu.SemaphoreType.DMA
-    grad_hidden, own, other = pl.pallas_call(
+    return pl.pallas_call(
         kernel,
-        out_shape=(
-            jax.ShapeDtypeStruct((TOK, FF), BF16),
-            jax.ShapeDtypeStruct((FF, D // 2), BF16),
-            jax.ShapeDtypeStruct((FF, D // 2), BF16),
-        ),
+        out_shape=(pltpu.VMEM((TOK, FF), BF16), pltpu.VMEM((FF, D // 2), F32)),
         in_specs=[anywhere, vmem, vmem, vmem, anywhere],
-        out_specs=(anywhere, anywhere, anywhere),
+        out_specs=(vmem, vmem),
         scratch_shapes=[
             pltpu.VMEM((FF, D), BF16),
             pltpu.VMEM((8, TOK, A), BF16),
@@ -268,20 +260,19 @@
             pltpu.VMEM((4, TOK, B), BF16),
             pltpu.VMEM((2, TOK, BH), BF16),
             pltpu.VMEM((2, TOK, B), BF16),
-            pltpu.VMEM((NG, 2, GT, D // 2), BF16),
+            pltpu.VMEM((NG, GT, D // 2), BF16),
+            pltpu.VMEM((NG, GT, D // 2), BF16),
             dma((MESSAGES,)),
             dma((MESSAGES,)),
             dma((NG,)),
             dma((NG,)),
-            dma((NG,)),
-            dma((5,)),
+            dma((3,)),
         ],
         compiler_params=pltpu.CompilerParams(
-            collective_id=0, has_side_effects=True, vmem_limit_bytes=56 * 2**20
+            collective_id=0, has_side_effects=True, vmem_limit_bytes=54 * 2**20
         ),
         cost_estimate=pl.CostEstimate(flops=4 * 1024 * FF * D, bytes_accessed=24 * 2**20, transcendentals=32),
     )(hidden, cotangent, language.reshape(1, TOK), counts.reshape(1, 32), weight)
-    return grad_hidden, own.astype(F32) + other.astype(F32)
 
 
 def solution(mesh):

time: 117 us -> 112 us (0.957)
  other arithmetic: 7.39 us -> 0 us
  local copies, waits for them, and re-layouts: 0.93 us -> 3.97 us
    add x1 -> x0, other arithmetic: 7.39 us -> none  [body(): return (grad_hidden, own.astype(F32) + other.astype(F32))]
    unnamed x3 -> x2, local copies, waits for them, and re-layouts: 0.93 us -> 3.97 us
where the time goes in v2:
time: 112 us; the launch traced here: 111 us
  Pallas kernels  106 us (95%)
  local copies, waits for them, and re-layouts  3.97 us (4%)
    pallas_call x1, Pallas kernels, body(): pl.pallas_call(kernel, out_shape=(pltpu.VMEM((TOK, FF), BF16), pltpu.VMEM...  106 us
    unnamed x2, local copies, waits for them, and re-layouts  3.97 us

profile of v2, /device:TPU:2, one launch (start us, length us, event | category | flops | bytes accessed | tf_op | source)
XLA Modules:
  0.0 110.7 jit_solution(558715836575909121)
XLA Ops:
  0.6 106.0 %shard_map.68 = (bf16[128,3584]{1,0:T(8,128)(2,1)S(1)}, f32[3584,512]{1,0:T(8,128)S(1)}) custom-call(bf16[128,3584]{1,0:T(8,128)(2,1)} %h_ref.1, bf16[128,1024]{1,0:T(8,128)(2,1)} %c_ref.1, s32[1,128]{1,0:T(1,128)} %bitcast.2, s32[1,32]{1,0:T(1,128)} %bitcast.3, bf16[3584,1024]{1,0:T(8,128)(2,1)} %w_ref.1), custom_call_target="tpu_custom_call" | custom-call | flops 15032385536 | bytes 25165824 | tf_op jit(solution)/shard_map/pallas_call | solution.py:245
  106.7 0.9 copy.9
  107.6 3.0 %copy.10 = f32[3584,512]{1,0:T(8,128)} copy(f32[3584,512]{1,0:T(8,128)S(1)} %get-tuple-element.3) | data formatting | bytes 14680064

commit v3 on v0

v3 whole, which is shorter than its diff:
```python
import jax
import jax.numpy as jnp
from jax import lax
from jax.experimental import pallas as pl
from jax.experimental.pallas import tpu as pltpu
from jax.sharding import PartitionSpec as P

MESH = pl.DeviceIdType.MESH
BF16 = jnp.bfloat16
F32 = jnp.float32

TOK = 128
FF = 3584
D = 1024
DH = D // 2
A = 1536
S = 1024
FT = 512
GT = 256
NA, NS = A // GT, S // GT
NW = 2
WR = S // 2 // NW
MESSAGES = 80


def column(row_vector, n):
    on_diagonal = lax.broadcasted_iota(jnp.int32, (n, n), 0) == lax.broadcasted_iota(jnp.int32, (n, n), 1)
    return jnp.sum(jnp.where(on_diagonal, jnp.broadcast_to(row_vector, (n, n)), 0.0), axis=1, keepdims=True)


def kernel(
    h_ref, c_ref, lang_ref, counts_ref, w_ref,
    gh_ref, gw_ref,
    wa, ws, wx, ha, hs, call, pa, ps, ra2, rs2, ra1, rs1, rax, rsx, gst, grv, xst, xrv, xsum, xin,
    ss, rs, gss, grs, xss, xrs, ls,
):
    dp, row, col = lax.axis_index("dp"), lax.axis_index("row"), lax.axis_index("col")
    xl, y = row // 4, row % 4
    z, h = col // 2, col % 2
    q = 1 - h
    x = h * 2 + xl
    xp, xm, xo = (x + 1) % 4, (x + 3) % 4, (x + 2) % 4
    zp, zm, zo = (z + 1) % 4, (z + 3) % 4, (z + 2) % 4
    yp, ym, yo = (y + 1) % 4, (y + 3) % 4, (y + 2) % 4

    def device(at_x, at_y, at_z):
        return (dp, (at_x % 2) * 4 + at_y, at_z * 2 + at_x // 2)

    to_zp, to_zm = device(x, y, zp), device(x, y, zm)
    to_yp, to_ym = device(x, yp, z), device(x, ym, z)
    to_xp, to_xm, to_x2 = device(xp, y, z), device(xm, y, z), device(xo, y, z)
    to_dp = (1 - dp, row, col)
    neighbours = (to_zp, to_zm, to_yp, to_ym, to_xp, to_xm, to_x2, to_dp)

    barrier = pltpu.get_barrier_semaphore()
    for neighbour in neighbours:
        pl.semaphore_signal(barrier, inc=1, device_id=neighbour, device_id_type=MESH)

    s_own = pl.multiple_of(A + S * h, S // 2)
    s_other = pl.multiple_of(A + S * q, S // 2)
    h_a, h_s, h_o = (h_ref.at[:, pl.ds(at, n)] for at, n in ((0, A), (s_own, S), (s_other, S)))
    loads = [
        pltpu.make_async_copy(h_a, ha.at[col], ls.at[0]),
        pltpu.make_async_copy(h_s, hs.at[col], ls.at[1]),
        pltpu.make_async_copy(w_ref.at[pl.ds(0, A), :], wa, ls.at[2]),
        pltpu.make_async_copy(w_ref.at[pl.ds(s_own, S), :], ws, ls.at[3]),
    ]
    for load in loads:
        load.start()

    lang_weight = column(jnp.sqrt(512.0 / counts_ref[...].astype(F32)), 32)
    matches = lang_ref[...] == lax.broadcasted_iota(jnp.int32, (32, TOK), 0)
    weight_row = jnp.sum(jnp.where(matches, lang_weight, 0.0), axis=0, keepdims=True)
    token_weight = column(weight_row, TOK)
    call[h, row] = (c_ref[...].astype(F32) * token_weight).astype(BF16)

    pl.semaphore_wait(barrier, len(neighbours))

    sent = []

    def send(src, dst, to):
        i = len(sent)
        copy = pltpu.make_async_remote_copy(
            src_ref=src, dst_ref=dst, send_sem=ss.at[i], recv_sem=rs.at[i], device_id=to, device_id_type=MESH
        )
        copy.start()
        sent.append(copy)
        return copy

    def got(*copies):
        for copy in copies:
            copy.wait_recv()

    def cots_whole(at_x, at_y, to):
        at = call.at[at_x // 2, (at_x % 2) * 4 + at_y]
        return send(at, at, to)

    def cots_half(at_x, at_y, half, to):
        at = call.at[at_x // 2, (at_x % 2) * 4 + at_y, pl.ds(half * (TOK // 2), TOK // 2), :]
        return send(at, at, to)

    def cots_along_y(at_x):
        return [cots_whole(at_x, y, to_yp), cots_whole(at_x, y, to_ym)]

    def cots_far_y(at_x):
        return [cots_half(at_x, ym, 0, to_yp), cots_half(at_x, yp, 1, to_ym)]

    def hidden_on(ref, hh, n):
        half = n // 2
        at_m, at_p = (ref.at[zz * 2 + hh, :, pl.ds(lo, half)] for zz, lo in ((zm, 0), (zp, half)))
        return [send(at_m, at_m, to_zp), send(at_p, at_p, to_zm)]

    def hidden_round(src, ref, at):
        return [send(src, ref.at[at], to_zp), send(src, ref.at[at], to_zm)]

    par = z * 2 + q
    c_x = [cots_whole(x, y, to_xp), cots_whole(x, y, to_xm)]
    own_a = hidden_round(h_a, ha, col)
    x_a = send(h_a, ha.at[col], to_x2)
    c_y = cots_along_y(x)
    own_s = hidden_round(h_s, hs, col)
    x_s = send(h_o, hs.at[col], to_x2)

    got(*c_x)
    c_x2 = [cots_half(xm, y, 0, to_xp), cots_half(xp, y, 1, to_xm)]
    c_ym, c_yp = cots_along_y(xm), cots_along_y(xp)
    got(*c_y)
    c_y2 = cots_far_y(x)
    got(*own_a)
    far_own_a = hidden_on(ha, h, A)
    got(x_a)
    par_a = hidden_round(ha.at[par], ha, par)
    got(*c_x2)
    c_yo = cots_along_y(xo)
    got(*own_s)
    far_own_s = hidden_on(hs, h, S)
    got(x_s)
    par_s = hidden_round(hs.at[par], hs, par)
    w_x = []
    for i in range(NW):
        rows = pl.multiple_of(dp * (S // 2) + i * WR, WR)
        w_x.append(send(w_ref.at[pl.ds(pl.multiple_of(s_other + rows, WR), WR), :], wx.at[pl.ds(rows, WR), :], to_x2))
    got(*c_ym)
    c_ym2 = cots_far_y(xm)
    got(*c_yp)
    c_yp2 = cots_far_y(xp)
    got(*par_a)
    far_par_a = hidden_on(ha, q, A)
    got(*c_yo)
    c_yo2 = cots_far_y(xo)
    for load in loads:
        load.wait()
    got(*par_s)
    far_par_s = hidden_on(hs, q, S)
    got(*c_y2, *c_ym2, *c_yp2, *c_yo2)

    def times_weight(cots, weight):
        return lax.dot_general(cots, weight, (((1,), (1,)), ((), ())), preferred_element_type=F32)

    def cots_of(hh, zd):
        return call[hh, pl.ds(zd * 2, 2)].reshape(2 * TOK, D)

    def terms_a(at, zd):
        def step(j, carry):
            units = pl.ds(pl.multiple_of(j * FT, FT), FT)
            pa[at, :, :, units] = times_weight(cots_of(h, zd), wa[units, :]).astype(BF16).reshape(2, TOK, FT)
            return carry
        lax.fori_loop(0, A // FT, step, 0)

    def terms_s(at, zd):
        def step(j, carry):
            units = pl.ds(pl.multiple_of(j * FT, FT), FT)
            both = times_weight(cots_of(h, zd), ws[units, :]) + times_weight(cots_of(q, zd), wx[units, :])
            ps[at, :, :, units] = both.astype(BF16).reshape(2, TOK, FT)
            return carry
        lax.fori_loop(0, S // FT, step, 0)

    def add(ref, at, *others):
        total = ref[at].astype(F32)
        for other, other_at in others:
            total = total + other[other_at].astype(F32)
        ref[at] = total.astype(BF16)

    everything = slice(None)

    def far(p, r2, hh, n):
        half = n // 2
        return [
            send(p.at[0, hh, :, pl.ds(0, half)], r2.at[hh, 0], to_zp),
            send(p.at[0, hh, :, pl.ds(half, half)], r2.at[hh, 1], to_zm),
        ]

    def near(p, r2, r1, hh, n):
        half = n // 2
        add(p, (1, hh, everything, slice(0, half)), (r2, (hh, 0)))
        add(p, (2, hh, everything, slice(half, n)), (r2, (hh, 1)))
        return [send(p.at[1, hh], r1.at[hh, 0], to_zp), send(p.at[2, hh], r1.at[hh, 1], to_zm)]

    def home(p, r1, hh):
        add(p, (3, hh), (r1, (hh, 0)), (r1, (hh, 1)))

    terms_a(0, zo)
    far_aq = far(pa, ra2, q, A)
    far_ah = far(pa, ra2, h, A)
    terms_a(1, zp)
    terms_a(2, zm)
    w_dp = []
    for i in range(NW):
        got(w_x[i])
        rows = pl.ds(pl.multiple_of(dp * (S // 2) + i * WR, WR), WR)
        w_dp.append(send(wx.at[rows, :], wx.at[rows, :], to_dp))
    got(*w_dp)
    terms_s(0, zo)
    far_sq = far(ps, rs2, q, S)
    far_sh = far(ps, rs2, h, S)
    got(*far_aq)
    near_aq = near(pa, ra2, ra1, q, A)
    terms_s(1, zp)
    terms_s(2, zm)

    def product(ref, j, hh, part):
        hidden = ref[:, :, pl.ds(pl.multiple_of(j * GT, GT), GT)].reshape(8 * TOK, GT)
        cots = call[hh, :, :, pl.ds(pl.multiple_of(part * DH, DH), DH)].reshape(8 * TOK, DH)
        out = lax.dot_general(hidden, cots, (((0,), (0,)), ((), ())), preferred_element_type=F32)
        return out.astype(BF16)

    def to_other_core(st, rv, s_sem, r_sem, j):
        return pltpu.make_async_remote_copy(
            src_ref=st.at[j], dst_ref=rv.at[j], send_sem=s_sem.at[j], recv_sem=r_sem.at[j],
            device_id=to_dp, device_id_type=MESH,
        )

    def partner_tile(j, carry):
        xst[j] = product(hs, j, q, 1 - dp)
        to_other_core(xst, xrv, xss, xrs, j).start()
        xsum[j] = product(hs, j, q, dp)
        return carry

    def own_tiles(ref, base, first, n):
        def step(j, carry):
            gst[base + j] = product(ref, j, h, 1 - dp)
            to_other_core(gst, grv, gss, grs, base + j).start()
            gw_ref[pl.ds(pl.multiple_of(first + j * GT, GT), GT), :] = product(ref, j, h, dp).astype(F32)
            return carry
        lax.fori_loop(0, n, step, 0)

    def own_sums(base, first, n):
        def step(j, carry):
            to_other_core(gst, grv, gss, grs, base + j).wait()
            gw_ref[pl.ds(pl.multiple_of(first + j * GT, GT), GT), :] += grv[base + j].astype(F32)
            return carry
        lax.fori_loop(0, n, step, 0)

    got(*far_own_s, *far_par_s)
    lax.fori_loop(0, NS, partner_tile, 0)
    got(*far_sq)
    near_sq = near(ps, rs2, rs1, q, S)
    got(*far_ah)
    near_ah = near(pa, ra2, ra1, h, A)
    returns = []
    for j in range(NS):
        to_other_core(xst, xrv, xss, xrs, j).wait()
        add(xsum, j, (xrv, j))
        returns.append(send(xsum.at[j], xin.at[j], to_x2))
    got(*far_sh)
    near_sh = near(ps, rs2, rs1, h, S)
    terms_a(3, z)
    terms_s(3, z)
    got(*far_own_a, *far_par_a)
    own_tiles(hs, NA, s_own, NS)
    got(*near_aq)
    home(pa, ra1, q)
    last_a = send(pa.at[3, q], rax, to_x2)
    own_tiles(ha, 0, 0, NA)
    got(*near_sq)
    home(ps, rs1, q)
    last_s = send(ps.at[3, q], rsx, to_x2)
    own_sums(0, 0, NA)
    own_sums(NA, s_own, NS)
    got(*near_ah)
    home(pa, ra1, h)
    for j in range(NS):
        got(returns[j])
        gw_ref[pl.ds(pl.multiple_of(s_other + j * GT, GT), GT), :] = xin[j].astype(F32)
    got(*near_sh)
    home(ps, rs1, h)
    gh_ref[:, pl.ds(s_own, S)] = ps[3, h]
    got(last_a)
    add(pa, (3, h), (rax, everything))
    gh_ref[:, 0:A] = pa[3, h]
    got(last_s)
    gh_ref[:, pl.ds(s_other, S)] = rsx[...]

    for copy in sent:
        copy.wait_send()


def body(hidden, cotangent, language, counts, weight):
    anywhere = pl.BlockSpec(memory_space=pl.ANY)
    vmem = pl.BlockSpec(memory_space=pltpu.VMEM)
    dma = pltpu.SemaphoreType.DMA
    return pl.pallas_call(
        kernel,
        out_shape=(pltpu.VMEM((TOK, FF), BF16), pltpu.VMEM((FF, DH), F32)),
        in_specs=[anywhere, vmem, vmem, vmem, anywhere],
        out_specs=(vmem, vmem),
        scratch_shapes=[
            pltpu.VMEM((A, D), BF16),
            pltpu.VMEM((S, D), BF16),
            pltpu.VMEM((S, D), BF16),
            pltpu.VMEM((8, TOK, A), BF16),
            pltpu.VMEM((8, TOK, S), BF16),
            pltpu.VMEM((2, 8, TOK, D), BF16),
            pltpu.VMEM((4, 2, TOK, A), BF16),
            pltpu.VMEM((4, 2, TOK, S), BF16),
            pltpu.VMEM((2, 2, TOK, A // 2), BF16),
            pltpu.VMEM((2, 2, TOK, S // 2), BF16),
            pltpu.VMEM((2, 2, TOK, A), BF16),
            pltpu.VMEM((2, 2, TOK, S), BF16),
            pltpu.VMEM((TOK, A), BF16),
            pltpu.VMEM((TOK, S), BF16),
            pltpu.VMEM((NA + NS, GT, DH), BF16),
            pltpu.VMEM((NA + NS, GT, DH), BF16),
            pltpu.VMEM((NS, GT, DH), BF16),
            pltpu.VMEM((NS, GT, DH), BF16),
            pltpu.VMEM((NS, GT, DH), BF16),
            pltpu.VMEM((NS, GT, DH), BF16),
            dma((MESSAGES,)),
            dma((MESSAGES,)),
            dma((NA + NS,)),
            dma((NA + NS,)),
            dma((NS,)),
            dma((NS,)),
            dma((4,)),
        ],
        compiler_params=pltpu.CompilerParams(
            collective_id=0, has_side_effects=True, vmem_limit_bytes=54 * 2**20
        ),
        cost_estimate=pl.CostEstimate(flops=4 * 1024 * FF * D, bytes_accessed=24 * 2**20, transcendentals=32),
    )(hidden, cotangent, language.reshape(1, TOK), counts.reshape(1, 32), weight)


def solution(mesh):
    placed = (
        P(("dp", "col"), "row"),
        P(("dp", "row"), "col"),
        P(("dp", "row")),
        P(),
        P("row", "col"),
    )
    return jax.shard_map(
        body,
        mesh=mesh,
        in_specs=placed,
        out_specs=(P(("dp", "col"), "row"), P("row", ("col", "dp"))),
        check_vma=False,
    )
```

time: 613 us -> 112 us (0.18); the launches traced: 604 us -> 110 us
  waiting for transfers between devices: 371 us -> 0 us
  matrix products: 117 us -> 0 us
  Pallas kernels: 0 us -> 105 us
  starting transfers between devices: 85.7 us -> 0 us
  other arithmetic: 15.9 us -> 0 us
  between operations: 14.5 us -> 0.64 us
    ppermute x31 -> x0, waiting for transfers between devices: 371 us -> none  [shifted_2(): lax.ppermute(array, axis, [(i, (i + by) % devices) for i in range(devices)])]
    dot_general x16 -> x0, matrix products: 117 us -> none  [the longest x8 89.6 us: body(): lax.dot_general(moving_hidden, moving_cotan, (((0,), (0,)), ((), ())), pr...]
    pallas_call x0 -> x1, Pallas kernels: none -> 105 us  [body(): pl.pallas_call(kernel, out_shape=(pltpu.VMEM((TOK, FF), BF16), pltpu.VMEM...]
    ppermute x31 -> x0, starting transfers between devices: 85.6 us -> none  [shifted_2(): lax.ppermute(array, axis, [(i, (i + by) % devices) for i in range(devices)])]
    select_n x9 -> x0, other arithmetic: 7.57 us -> none  [the longest x3 4.5 us: body(): jnp.where(row_at >> bit_pos & 1 == 1, shifted, moving_hidden)]
    convert_element_type x2 -> x0, other arithmetic: 6.95 us -> none  [the longest x1 6.14 us: body(): grad_weight = lax.psum_scatter(weight_grad.astype(jnp.bfloat16), 'dp', sc...]
  transfers between devices with their start and end apart: 32 -> 0, of which waited for: 23 -> 0; matrix products, arithmetic and copies ran while one was open for 20% -> 0% of each run, Pallas kernels for 0% -> 0%
where the time goes in v3:
time: 112 us; the launch traced here: 110 us
  Pallas kernels  105 us (94%)
  local copies, waits for them, and re-layouts  3.97 us (4%)
    pallas_call x1, Pallas kernels, body(): pl.pallas_call(kernel, out_shape=(pltpu.VMEM((TOK, FF), BF16), pltpu.VMEM...  105 us
    unnamed x2, local copies, waits for them, and re-layouts  3.97 us

profile of v3, /device:TPU:2, one launch (start us, length us, event | category | flops | bytes accessed | tf_op | source)
XLA Modules:
  0.0 110.1 jit_solution(10745046547657351250)
XLA Ops:
  0.6 105.5 %shard_map.68 = (bf16[128,3584]{1,0:T(8,128)(2,1)S(1)}, f32[3584,512]{1,0:T(8,128)S(1)}) custom-call(bf16[128,3584]{1,0:T(8,128)(2,1)} %h_ref.1, bf16[128,1024]{1,0:T(8,128)(2,1)} %c_ref.1, s32[1,128]{1,0:T(1,128)} %bitcast.2, s32[1,32]{1,0:T(1,128)} %bitcast.3, bf16[3584,1024]{1,0:T(8,128)(2,1)} %w_ref.1), custom_call_target="tpu_custom_call" | custom-call | flops 15032385536 | bytes 25165824 | tf_op jit(solution)/shard_map/pallas_call | solution.py:302
  106.1 0.9 copy.9
  107.1 3.0 %copy.10 = f32[3584,512]{1,0:T(8,128)} copy(f32[3584,512]{1,0:T(8,128)S(1)} %get-tuple-element.3) | data formatting | bytes 14680064

commit v4 on v3

--- a/solution.py
+++ b/solution.py
@@ -115,43 +115,43 @@
 
     par = z * 2 + q
     c_x = [cots_whole(x, y, to_xp), cots_whole(x, y, to_xm)]
+    own_s = hidden_round(h_s, hs, col)
+    c_y = cots_along_y(x)
+    x_s = send(h_o, hs.at[col], to_x2)
     own_a = hidden_round(h_a, ha, col)
-    x_a = send(h_a, ha.at[col], to_x2)
-    c_y = cots_along_y(x)
-    own_s = hidden_round(h_s, hs, col)
-    x_s = send(h_o, hs.at[col], to_x2)
 
     got(*c_x)
     c_x2 = [cots_half(xm, y, 0, to_xp), cots_half(xp, y, 1, to_xm)]
     c_ym, c_yp = cots_along_y(xm), cots_along_y(xp)
-    got(*c_y)
-    c_y2 = cots_far_y(x)
-    got(*own_a)
-    far_own_a = hidden_on(ha, h, A)
-    got(x_a)
-    par_a = hidden_round(ha.at[par], ha, par)
-    got(*c_x2)
-    c_yo = cots_along_y(xo)
-    got(*own_s)
-    far_own_s = hidden_on(hs, h, S)
-    got(x_s)
-    par_s = hidden_round(hs.at[par], hs, par)
+    x_a = send(h_a, ha.at[col], to_x2)
     w_x = []
     for i in range(NW):
         rows = pl.multiple_of(dp * (S // 2) + i * WR, WR)
         w_x.append(send(w_ref.at[pl.ds(pl.multiple_of(s_other + rows, WR), WR), :], wx.at[pl.ds(rows, WR), :], to_x2))
+    got(*own_s)
+    far_own_s = hidden_on(hs, h, S)
+    got(*c_y)
+    c_y2 = cots_far_y(x)
+    got(x_s)
+    par_s = hidden_round(hs.at[par], hs, par)
+    got(*c_x2)
+    c_yo = cots_along_y(xo)
+    got(*own_a)
     got(*c_ym)
     c_ym2 = cots_far_y(xm)
     got(*c_yp)
     c_yp2 = cots_far_y(xp)
-    got(*par_a)
-    far_par_a = hidden_on(ha, q, A)
+    got(*par_s)
+    far_par_s = hidden_on(hs, q, S)
+    got(x_a)
+    par_a = hidden_round(ha.at[par], ha, par)
+    far_own_a = hidden_on(ha, h, A)
     got(*c_yo)
     c_yo2 = cots_far_y(xo)
     for load in loads:
         load.wait()
-    got(*par_s)
-    far_par_s = hidden_on(hs, q, S)
+    got(*par_a)
+    far_par_a = hidden_on(ha, q, A)
     got(*c_y2, *c_ym2, *c_yp2, *c_yo2)
 
     def times_weight(cots, weight):
@@ -199,11 +199,58 @@
     def home(p, r1, hh):
         add(p, (3, hh), (r1, (hh, 0)), (r1, (hh, 1)))
 
+    def product(ref, j, hh, part):
+        hidden = ref[:, :, pl.ds(j * GT if isinstance(j, int) else pl.multiple_of(j * GT, GT), GT)].reshape(8 * TOK, GT)
+        cots = call[hh, :, :, pl.ds(pl.multiple_of(part * DH, DH), DH)].reshape(8 * TOK, DH)
+        out = lax.dot_general(hidden, cots, (((0,), (0,)), ((), ())), preferred_element_type=F32)
+        return out.astype(BF16)
+
+    def to_other_core(st, rv, s_sem, r_sem, j):
+        return pltpu.make_async_remote_copy(
+            src_ref=st.at[j], dst_ref=rv.at[j], send_sem=s_sem.at[j], recv_sem=r_sem.at[j],
+            device_id=to_dp, device_id_type=MESH,
+        )
+
+    def partner_tile(j):
+        xst[j] = product(hs, j, q, 1 - dp)
+        to_other_core(xst, xrv, xss, xrs, j).start()
+        xsum[j] = product(hs, j, q, dp)
+
+    def own_tiles(ref, base, first, n, start=0):
+        def step(j, carry):
+            gst[base + j] = product(ref, j, h, 1 - dp)
+            to_other_core(gst, grv, gss, grs, base + j).start()
+            gw_ref[pl.ds(pl.multiple_of(first + j * GT, GT), GT), :] = product(ref, j, h, dp).astype(F32)
+            return carry
+        lax.fori_loop(start, n, step, 0)
+
+    def own_sums(base, first, n):
+        def step(j, carry):
+            to_other_core(gst, grv, gss, grs, base + j).wait()
+            gw_ref[pl.ds(pl.multiple_of(first + j * GT, GT), GT), :] += grv[base + j].astype(F32)
+            return carry
+        lax.fori_loop(0, n, step, 0)
+
     terms_a(0, zo)
     far_aq = far(pa, ra2, q, A)
     far_ah = far(pa, ra2, h, A)
+    got(*far_own_s, *far_par_s)
+    returns = []
+
+    def give_back(j):
+        to_other_core(xst, xrv, xss, xrs, j).wait()
+        add(xsum, j, (xrv, j))
+        returns.append(send(xsum.at[j], xin.at[j], to_x2))
+
+    for j in range(NS):
+        partner_tile(j)
+        if j:
+            give_back(j - 1)
+    give_back(NS - 1)
     terms_a(1, zp)
     terms_a(2, zm)
+    got(*far_aq)
+    near_aq = near(pa, ra2, ra1, q, A)
     w_dp = []
     for i in range(NW):
         got(w_x[i])
@@ -213,68 +260,26 @@
     terms_s(0, zo)
     far_sq = far(ps, rs2, q, S)
     far_sh = far(ps, rs2, h, S)
-    got(*far_aq)
-    near_aq = near(pa, ra2, ra1, q, A)
     terms_s(1, zp)
     terms_s(2, zm)
-
-    def product(ref, j, hh, part):
-        hidden = ref[:, :, pl.ds(pl.multiple_of(j * GT, GT), GT)].reshape(8 * TOK, GT)
-        cots = call[hh, :, :, pl.ds(pl.multiple_of(part * DH, DH), DH)].reshape(8 * TOK, DH)
-        out = lax.dot_general(hidden, cots, (((0,), (0,)), ((), ())), preferred_element_type=F32)
-        return out.astype(BF16)
-
-    def to_other_core(st, rv, s_sem, r_sem, j):
-        return pltpu.make_async_remote_copy(
-            src_ref=st.at[j], dst_ref=rv.at[j], send_sem=s_sem.at[j], recv_sem=r_sem.at[j],
-            device_id=to_dp, device_id_type=MESH,
-        )
-
-    def partner_tile(j, carry):
-        xst[j] = product(hs, j, q, 1 - dp)
-        to_other_core(xst, xrv, xss, xrs, j).start()
-        xsum[j] = product(hs, j, q, dp)
-        return carry
-
-    def own_tiles(ref, base, first, n):
-        def step(j, carry):
-            gst[base + j] = product(ref, j, h, 1 - dp)
-            to_other_core(gst, grv, gss, grs, base + j).start()
-            gw_ref[pl.ds(pl.multiple_of(first + j * GT, GT), GT), :] = product(ref, j, h, dp).astype(F32)
-            return carry
-        lax.fori_loop(0, n, step, 0)
-
-    def own_sums(base, first, n):
-        def step(j, carry):
-            to_other_core(gst, grv, gss, grs, base + j).wait()
-            gw_ref[pl.ds(pl.multiple_of(first + j * GT, GT), GT), :] += grv[base + j].astype(F32)
-            return carry
-        lax.fori_loop(0, n, step, 0)
-
-    got(*far_own_s, *far_par_s)
-    lax.fori_loop(0, NS, partner_tile, 0)
+    got(*far_ah)
     got(*far_sq)
     near_sq = near(ps, rs2, rs1, q, S)
-    got(*far_ah)
     near_ah = near(pa, ra2, ra1, h, A)
-    returns = []
-    for j in range(NS):
-        to_other_core(xst, xrv, xss, xrs, j).wait()
-        add(xsum, j, (xrv, j))
-        returns.append(send(xsum.at[j], xin.at[j], to_x2))
     got(*far_sh)
     near_sh = near(ps, rs2, rs1, h, S)
     terms_a(3, z)
     terms_s(3, z)
-    got(*far_own_a, *far_par_a)
-    own_tiles(hs, NA, s_own, NS)
     got(*near_aq)
     home(pa, ra1, q)
     last_a = send(pa.at[3, q], rax, to_x2)
-    own_tiles(ha, 0, 0, NA)
+    got(*far_own_a, *far_par_a)
+    own_tiles(hs, NA, s_own, NS)
+    own_tiles(ha, 0, 0, 2)
     got(*near_sq)
     home(ps, rs1, q)
     last_s = send(ps.at[3, q], rsx, to_x2)
+    own_tiles(ha, 0, 0, NA, 2)
     own_sums(0, 0, NA)
     own_sums(NA, s_own, NS)
     got(*near_ah)
@@ -282,14 +287,14 @@
     for j in range(NS):
         got(returns[j])
         gw_ref[pl.ds(pl.multiple_of(s_other + j * GT, GT), GT), :] = xin[j].astype(F32)
-    got(*near_sh)
-    home(ps, rs1, h)
-    gh_ref[:, pl.ds(s_own, S)] = ps[3, h]
     got(last_a)
     add(pa, (3, h), (rax, everything))
     gh_ref[:, 0:A] = pa[3, h]
     got(last_s)
     gh_ref[:, pl.ds(s_other, S)] = rsx[...]
+    got(*near_sh)
+    home(ps, rs1, h)
+    gh_ref[:, pl.ds(s_own, S)] = ps[3, h]
 
     for copy in sent:
         copy.wait_send()

time: 112 us -> 101 us (0.902)
  Pallas kernels: 105 us -> 95.3 us
    pallas_call x1, Pallas kernels: 105 us -> 95.3 us  [body(): pl.pallas_call(kernel, out_shape=(pltpu.VMEM((TOK, FF), BF16), pltpu.VMEM...]
where the time goes in v4:
time: 101 us; the launch traced here: 100 us
  Pallas kernels  95.3 us (94%)
  local copies, waits for them, and re-layouts  3.97 us (4%)
    pallas_call x1, Pallas kernels, body(): pl.pallas_call(kernel, out_shape=(pltpu.VMEM((TOK, FF), BF16), pltpu.VMEM...  95.3 us
    unnamed x2, local copies, waits for them, and re-layouts  3.97 us

profile of v4, /device:TPU:2, one launch (start us, length us, event | category | flops | bytes accessed | tf_op | source)
XLA Modules:
  0.0 100.0 jit_solution(3931516375433070110)
XLA Ops:
  0.6 95.3 %shard_map.68 = (bf16[128,3584]{1,0:T(8,128)(2,1)S(1)}, f32[3584,512]{1,0:T(8,128)S(1)}) custom-call(bf16[128,3584]{1,0:T(8,128)(2,1)} %h_ref.1, bf16[128,1024]{1,0:T(8,128)(2,1)} %c_ref.1, s32[1,128]{1,0:T(1,128)} %bitcast.2, s32[1,32]{1,0:T(1,128)} %bitcast.3, bf16[3584,1024]{1,0:T(8,128)(2,1)} %w_ref.1), custom_call_target="tpu_custom_call" | custom-call | flops 15032385536 | bytes 25165824 | tf_op jit(solution)/shard_map/pallas_call | solution.py:307
  96.0 0.9 copy.9
  96.9 3.0 %copy.10 = f32[3584,512]{1,0:T(8,128)} copy(f32[3584,512]{1,0:T(8,128)S(1)} %get-tuple-element.3) | data formatting | bytes 14680064

commit v5 on v4

--- a/solution.py
+++ b/solution.py
@@ -20,7 +20,8 @@
 NA, NS = A // GT, S // GT
 NW = 2
 WR = S // 2 // NW
-MESSAGES = 80
+MESSAGES = 96
+PIECES = 7
 
 
 def column(row_vector, n):
@@ -31,7 +32,7 @@
 def kernel(
     h_ref, c_ref, lang_ref, counts_ref, w_ref,
     gh_ref, gw_ref,
-    wa, ws, wx, ha, hs, call, pa, ps, ra2, rs2, ra1, rs1, rax, rsx, gst, grv, xst, xrv, xsum, xin,
+    wa, ws, wx, ha, hs, call, pa, ps, ra2, rs2, ra1, rs1, rax, rsx, gst, grv, xst, xrv, xsum, xin, lang, counts, cin,
     ss, rs, gss, grs, xss, xrs, ls,
 ):
     dp, row, col = lax.axis_index("dp"), lax.axis_index("row"), lax.axis_index("col")
@@ -59,20 +60,27 @@
     s_own = pl.multiple_of(A + S * h, S // 2)
     s_other = pl.multiple_of(A + S * q, S // 2)
     h_a, h_s, h_o = (h_ref.at[:, pl.ds(at, n)] for at, n in ((0, A), (s_own, S), (s_other, S)))
+    small = [
+        pltpu.make_async_copy(lang_ref, lang, ls.at[4]),
+        pltpu.make_async_copy(counts_ref, counts, ls.at[5]),
+        pltpu.make_async_copy(c_ref, cin, ls.at[6]),
+    ]
     loads = [
         pltpu.make_async_copy(h_a, ha.at[col], ls.at[0]),
         pltpu.make_async_copy(h_s, hs.at[col], ls.at[1]),
         pltpu.make_async_copy(w_ref.at[pl.ds(0, A), :], wa, ls.at[2]),
         pltpu.make_async_copy(w_ref.at[pl.ds(s_own, S), :], ws, ls.at[3]),
     ]
-    for load in loads:
+    for load in small + loads:
         load.start()
-
-    lang_weight = column(jnp.sqrt(512.0 / counts_ref[...].astype(F32)), 32)
-    matches = lang_ref[...] == lax.broadcasted_iota(jnp.int32, (32, TOK), 0)
+    for load in small:
+        load.wait()
+
+    lang_weight = column(jnp.sqrt(512.0 / counts[...].astype(F32)), 32)
+    matches = lang[...] == lax.broadcasted_iota(jnp.int32, (32, TOK), 0)
     weight_row = jnp.sum(jnp.where(matches, lang_weight, 0.0), axis=0, keepdims=True)
     token_weight = column(weight_row, TOK)
-    call[h, row] = (c_ref[...].astype(F32) * token_weight).astype(BF16)
+    call[h, row] = (cin[...].astype(F32) * token_weight).astype(BF16)
 
     pl.semaphore_wait(barrier, len(neighbours))
 
@@ -109,6 +117,10 @@
         half = n // 2
         at_m, at_p = (ref.at[zz * 2 + hh, :, pl.ds(lo, half)] for zz, lo in ((zm, 0), (zp, half)))
         return [send(at_m, at_m, to_zp), send(at_p, at_p, to_zm)]
+
+    def hidden_halves(ref, at, n):
+        lo, hi = ref.at[at, :, pl.ds(0, n // 2)], ref.at[at, :, pl.ds(n // 2, n // 2)]
+        return [send(lo, lo, to_zp), send(hi, hi, to_zm)], [send(hi, hi, to_zp), send(lo, lo, to_zm)]
 
     def hidden_round(src, ref, at):
         return [send(src, ref.at[at], to_zp), send(src, ref.at[at], to_zm)]
@@ -137,6 +149,7 @@
     got(*c_x2)
     c_yo = cots_along_y(xo)
     got(*own_a)
+    far_own_a = hidden_on(ha, h, A)
     got(*c_ym)
     c_ym2 = cots_far_y(xm)
     got(*c_yp)
@@ -144,8 +157,7 @@
     got(*par_s)
     far_par_s = hidden_on(hs, q, S)
     got(x_a)
-    par_a = hidden_round(ha.at[par], ha, par)
-    far_own_a = hidden_on(ha, h, A)
+    par_a, par_a2 = hidden_halves(ha, par, A)
     got(*c_yo)
     c_yo2 = cots_far_y(xo)
     for load in loads:
@@ -249,31 +261,31 @@
     give_back(NS - 1)
     terms_a(1, zp)
     terms_a(2, zm)
-    got(*far_aq)
-    near_aq = near(pa, ra2, ra1, q, A)
+    terms_a(3, z)
     w_dp = []
     for i in range(NW):
         got(w_x[i])
         rows = pl.ds(pl.multiple_of(dp * (S // 2) + i * WR, WR), WR)
         w_dp.append(send(wx.at[rows, :], wx.at[rows, :], to_dp))
+    got(*far_aq)
+    near_aq = near(pa, ra2, ra1, q, A)
     got(*w_dp)
     terms_s(0, zo)
     far_sq = far(ps, rs2, q, S)
     far_sh = far(ps, rs2, h, S)
     terms_s(1, zp)
     terms_s(2, zm)
-    got(*far_ah)
+    got(*near_aq)
+    home(pa, ra1, q)
+    last_a = send(pa.at[3, q], rax, to_x2)
     got(*far_sq)
     near_sq = near(ps, rs2, rs1, q, S)
+    got(*far_ah)
     near_ah = near(pa, ra2, ra1, h, A)
     got(*far_sh)
     near_sh = near(ps, rs2, rs1, h, S)
-    terms_a(3, z)
     terms_s(3, z)
-    got(*near_aq)
-    home(pa, ra1, q)
-    last_a = send(pa.at[3, q], rax, to_x2)
-    got(*far_own_a, *far_par_a)
+    got(*far_own_a, *par_a2, *far_par_a)
     own_tiles(hs, NA, s_own, NS)
     own_tiles(ha, 0, 0, 2)
     got(*near_sq)
@@ -300,14 +312,26 @@
         copy.wait_send()
 
 
+def write_out(gh_ref, gw_ref, gh_out, gw_out, sems):
+    rows = FF // PIECES
+    copies = [pltpu.make_async_copy(gh_ref, gh_out, sems.at[PIECES])]
+    for i in range(PIECES):
+        at = pl.ds(i * rows, rows)
+        copies.append(pltpu.make_async_copy(gw_ref.at[at, :], gw_out.at[at, :], sems.at[i]))
+    for copy in copies:
+        copy.start()
+    for copy in copies:
+        copy.wait()
+
+
 def body(hidden, cotangent, language, counts, weight):
     anywhere = pl.BlockSpec(memory_space=pl.ANY)
     vmem = pl.BlockSpec(memory_space=pltpu.VMEM)
     dma = pltpu.SemaphoreType.DMA
-    return pl.pallas_call(
+    results = pl.pallas_call(
         kernel,
         out_shape=(pltpu.VMEM((TOK, FF), BF16), pltpu.VMEM((FF, DH), F32)),
-        in_specs=[anywhere, vmem, vmem, vmem, anywhere],
+        in_specs=[anywhere] * 5,
         out_specs=(vmem, vmem),
         scratch_shapes=[
             pltpu.VMEM((A, D), BF16),
@@ -330,19 +354,30 @@
             pltpu.VMEM((NS, GT, DH), BF16),
             pltpu.VMEM((NS, GT, DH), BF16),
             pltpu.VMEM((NS, GT, DH), BF16),
+            pltpu.VMEM((1, TOK), jnp.int32),
+            pltpu.VMEM((1, 32), jnp.int32),
+            pltpu.VMEM((TOK, D), BF16),
             dma((MESSAGES,)),
             dma((MESSAGES,)),
             dma((NA + NS,)),
             dma((NA + NS,)),
             dma((NS,)),
             dma((NS,)),
-            dma((4,)),
+            dma((7,)),
         ],
         compiler_params=pltpu.CompilerParams(
             collective_id=0, has_side_effects=True, vmem_limit_bytes=54 * 2**20
         ),
         cost_estimate=pl.CostEstimate(flops=4 * 1024 * FF * D, bytes_accessed=24 * 2**20, transcendentals=32),
     )(hidden, cotangent, language.reshape(1, TOK), counts.reshape(1, 32), weight)
+    return pl.pallas_call(
+        write_out,
+        out_shape=(jax.ShapeDtypeStruct((TOK, FF), BF16), jax.ShapeDtypeStruct((FF, DH), F32)),
+        in_specs=[vmem, vmem],
+        out_specs=(anywhere, anywhere),
+        scratch_shapes=[dma((PIECES + 1,))],
+        compiler_params=pltpu.CompilerParams(vmem_limit_bytes=2**20),
+    )(*results)
 
 
 def solution(mesh):

time: 101 us -> 98.7 us (0.977)
  local copies, waits for them, and re-layouts: 3.97 us -> 0 us
  Pallas kernels: 95.3 us -> 97.8 us
    unnamed x2 -> x0, local copies, waits for them, and re-layouts: 3.97 us -> none
    pallas_call x0 -> x1, Pallas kernels: none -> 3.35 us  [body(): pl.pallas_call(write_out, out_shape=(jax.ShapeDtypeStruct((TOK, FF), BF16...]
where the time goes in v5:
time: 98.7 us; the launch traced here: 98.4 us
  Pallas kernels  97.8 us (99%)
    pallas_call x1, Pallas kernels, body(): pl.pallas_call(kernel, out_shape=(pltpu.VMEM((TOK, FF), BF16), pltpu.VMEM...  94.4 us
    pallas_call x1, Pallas kernels, body(): pl.pallas_call(write_out, out_shape=(jax.ShapeDtypeStruct((TOK, FF), BF16...  3.35 us

profile of v5, /device:TPU:2, one launch (start us, length us, event | category | flops | bytes accessed | tf_op | source)
XLA Modules:
  0.0 98.4 jit_solution(1282096695719437510)
XLA Ops:
  0.6 94.4 %shard_map.68 = (bf16[128,3584]{1,0:T(8,128)(2,1)S(1)}, f32[3584,512]{1,0:T(8,128)S(1)}) custom-call(bf16[128,3584]{1,0:T(8,128)(2,1)} %h_ref.1, bf16[128,1024]{1,0:T(8,128)(2,1)} %c_ref.1, s32[1,128]{1,0:T(1,128)} %bitcast.2, s32[1,32]{1,0:T(1,128)} %bitcast.3, bf16[3584,1024]{1,0:T(8,128)(2,1)} %w_ref.1), custom_call_target="tpu_custom_call" | custom-call | flops 15032385536 | bytes 25165824 | tf_op jit(solution)/shard_map/pallas_call | solution.py:331
  95.1 3.4 %shard_map.69 = (bf16[128,3584]{1,0:T(8,128)(2,1)}, f32[3584,512]{1,0:T(8,128)}) custom-call(bf16[128,3584]{1,0:T(8,128)(2,1)S(1)} %get-tuple-element.4.gh_ref, f32[3584,512]{1,0:T(8,128)S(1)} %get-tuple-element.5.gw_ref), custom_call_target="tpu_custom_call" | custom-call | tf_op jit(solution)/shard_map/pallas_call | solution.py:373

commit v6 on v5

--- a/solution.py
+++ b/solution.py
@@ -13,11 +13,11 @@
 FF = 3584
 D = 1024
 DH = D // 2
-A = 1536
-S = 1024
+A, S = 1536, 1024
+AW, SW = 1280, 1152
 FT = 512
-GT = 256
-NA, NS = A // GT, S // GT
+TA, TS = 256, 384
+NA, NS = AW // TA, SW // TS
 NW = 2
 WR = S // 2 // NW
 MESSAGES = 96
@@ -32,8 +32,8 @@
 def kernel(
     h_ref, c_ref, lang_ref, counts_ref, w_ref,
     gh_ref, gw_ref,
-    wa, ws, wx, ha, hs, call, pa, ps, ra2, rs2, ra1, rs1, rax, rsx, gst, grv, xst, xrv, xsum, xin, lang, counts, cin,
-    ss, rs, gss, grs, xss, xrs, ls,
+    wa, ws, wx, ha, hs, call, pa, ps, ra2, rs2, ra1, rs1, rax, rsx, gsa, gra, gss, grs, xst, xrv, xsum, xin, lang, counts, cin,
+    ss, rs, sem_a, sem_s, sem_x, ls,
 ):
     dp, row, col = lax.axis_index("dp"), lax.axis_index("row"), lax.axis_index("col")
     xl, y = row // 4, row % 4
@@ -59,7 +59,9 @@
 
     s_own = pl.multiple_of(A + S * h, S // 2)
     s_other = pl.multiple_of(A + S * q, S // 2)
-    h_a, h_s, h_o = (h_ref.at[:, pl.ds(at, n)] for at, n in ((0, A), (s_own, S), (s_other, S)))
+    sw_own = pl.multiple_of(AW + SW * h, 128)
+    sw_other = pl.multiple_of(AW + SW * q, 128)
+    h_a, h_s, h_o = (h_ref.at[:, pl.ds(at, n)] for at, n in ((0, AW), (sw_own, SW), (sw_other, SW)))
     small = [
         pltpu.make_async_copy(lang_ref, lang, ls.at[4]),
         pltpu.make_async_copy(counts_ref, counts, ls.at[5]),
@@ -113,9 +115,8 @@
     def cots_far_y(at_x):
         return [cots_half(at_x, ym, 0, to_yp), cots_half(at_x, yp, 1, to_ym)]
 
-    def hidden_on(ref, hh, n):
-        half = n // 2
-        at_m, at_p = (ref.at[zz * 2 + hh, :, pl.ds(lo, half)] for zz, lo in ((zm, 0), (zp, half)))
+    def hidden_on(ref, hh, n, cut):
+        at_m, at_p = ref.at[zm * 2 + hh, :, pl.ds(0, cut)], ref.at[zp * 2 + hh, :, pl.ds(cut, n - cut)]
         return [send(at_m, at_m, to_zp), send(at_p, at_p, to_zm)]
 
     def hidden_halves(ref, at, n):
@@ -141,7 +142,7 @@
         rows = pl.multiple_of(dp * (S // 2) + i * WR, WR)
         w_x.append(send(w_ref.at[pl.ds(pl.multiple_of(s_other + rows, WR), WR), :], wx.at[pl.ds(rows, WR), :], to_x2))
     got(*own_s)
-    far_own_s = hidden_on(hs, h, S)
+    far_own_s = hidden_on(hs, h, SW, 640)
     got(*c_y)
     c_y2 = cots_far_y(x)
     got(x_s)
@@ -149,21 +150,21 @@
     got(*c_x2)
     c_yo = cots_along_y(xo)
     got(*own_a)
-    far_own_a = hidden_on(ha, h, A)
+    far_own_a = hidden_on(ha, h, AW, AW // 2)
     got(*c_ym)
     c_ym2 = cots_far_y(xm)
     got(*c_yp)
     c_yp2 = cots_far_y(xp)
     got(*par_s)
-    far_par_s = hidden_on(hs, q, S)
+    far_par_s = hidden_on(hs, q, SW, 512)
     got(x_a)
-    par_a, par_a2 = hidden_halves(ha, par, A)
+    par_a, par_a2 = hidden_halves(ha, par, AW)
     got(*c_yo)
     c_yo2 = cots_far_y(xo)
     for load in loads:
         load.wait()
     got(*par_a)
-    far_par_a = hidden_on(ha, q, A)
+    far_par_a = hidden_on(ha, q, AW, AW // 2)
     got(*c_y2, *c_ym2, *c_yp2, *c_yo2)
 
     def times_weight(cots, weight):
@@ -211,35 +212,37 @@
     def home(p, r1, hh):
         add(p, (3, hh), (r1, (hh, 0)), (r1, (hh, 1)))
 
-    def product(ref, j, hh, part):
-        hidden = ref[:, :, pl.ds(j * GT if isinstance(j, int) else pl.multiple_of(j * GT, GT), GT)].reshape(8 * TOK, GT)
+    def product(ref, units, hh, part):
+        hidden = ref[:, :, units].reshape(8 * TOK, units.size)
         cots = call[hh, :, :, pl.ds(pl.multiple_of(part * DH, DH), DH)].reshape(8 * TOK, DH)
         out = lax.dot_general(hidden, cots, (((0,), (0,)), ((), ())), preferred_element_type=F32)
         return out.astype(BF16)
 
-    def to_other_core(st, rv, s_sem, r_sem, j):
+    def to_other_core(st, rv, sems, j):
         return pltpu.make_async_remote_copy(
-            src_ref=st.at[j], dst_ref=rv.at[j], send_sem=s_sem.at[j], recv_sem=r_sem.at[j],
+            src_ref=st.at[j], dst_ref=rv.at[j], send_sem=sems.at[0, j], recv_sem=sems.at[1, j],
             device_id=to_dp, device_id_type=MESH,
         )
 
     def partner_tile(j):
-        xst[j] = product(hs, j, q, 1 - dp)
-        to_other_core(xst, xrv, xss, xrs, j).start()
-        xsum[j] = product(hs, j, q, dp)
-
-    def own_tiles(ref, base, first, n, start=0):
+        units = pl.ds(j * TS, TS)
+        xst[j] = product(hs, units, q, 1 - dp)
+        to_other_core(xst, xrv, sem_x, j).start()
+        xsum[j] = product(hs, units, q, dp)
+
+    def own_tiles(ref, st, rv, sems, size, first, lo, hi):
         def step(j, carry):
-            gst[base + j] = product(ref, j, h, 1 - dp)
-            to_other_core(gst, grv, gss, grs, base + j).start()
-            gw_ref[pl.ds(pl.multiple_of(first + j * GT, GT), GT), :] = product(ref, j, h, dp).astype(F32)
+            units = pl.ds(pl.multiple_of(j * size, 128), size)
+            st[j] = product(ref, units, h, 1 - dp)
+            to_other_core(st, rv, sems, j).start()
+            gw_ref[pl.ds(pl.multiple_of(first + j * size, 128), size), :] = product(ref, units, h, dp).astype(F32)
             return carry
-        lax.fori_loop(start, n, step, 0)
-
-    def own_sums(base, first, n):
+        lax.fori_loop(lo, hi, step, 0)
+
+    def own_sums(st, rv, sems, size, first, n):
         def step(j, carry):
-            to_other_core(gst, grv, gss, grs, base + j).wait()
-            gw_ref[pl.ds(pl.multiple_of(first + j * GT, GT), GT), :] += grv[base + j].astype(F32)
+            to_other_core(st, rv, sems, j).wait()
+            gw_ref[pl.ds(pl.multiple_of(first + j * size, 128), size), :] += rv[j].astype(F32)
             return carry
         lax.fori_loop(0, n, step, 0)
 
@@ -250,7 +253,7 @@
     returns = []
 
     def give_back(j):
-        to_other_core(xst, xrv, xss, xrs, j).wait()
+        to_other_core(xst, xrv, sem_x, j).wait()
         add(xsum, j, (xrv, j))
         returns.append(send(xsum.at[j], xin.at[j], to_x2))
 
@@ -286,19 +289,19 @@
     near_sh = near(ps, rs2, rs1, h, S)
     terms_s(3, z)
     got(*far_own_a, *par_a2, *far_par_a)
-    own_tiles(hs, NA, s_own, NS)
-    own_tiles(ha, 0, 0, 2)
+    own_tiles(hs, gss, grs, sem_s, TS, sw_own, 0, NS)
+    own_tiles(ha, gsa, gra, sem_a, TA, 0, 0, 1)
     got(*near_sq)
     home(ps, rs1, q)
     last_s = send(ps.at[3, q], rsx, to_x2)
-    own_tiles(ha, 0, 0, NA, 2)
-    own_sums(0, 0, NA)
-    own_sums(NA, s_own, NS)
+    own_tiles(ha, gsa, gra, sem_a, TA, 0, 1, NA)
+    own_sums(gsa, gra, sem_a, TA, 0, NA)
+    own_sums(gss, grs, sem_s, TS, sw_own, NS)
     got(*near_ah)
     home(pa, ra1, h)
     for j in range(NS):
         got(returns[j])
-        gw_ref[pl.ds(pl.multiple_of(s_other + j * GT, GT), GT), :] = xin[j].astype(F32)
+        gw_ref[pl.ds(pl.multiple_of(sw_other + j * TS, 128), TS), :] = xin[j].astype(F32)
     got(last_a)
     add(pa, (3, h), (rax, everything))
     gh_ref[:, 0:A] = pa[3, h]
@@ -337,8 +340,8 @@
             pltpu.VMEM((A, D), BF16),
             pltpu.VMEM((S, D), BF16),
             pltpu.VMEM((S, D), BF16),
-            pltpu.VMEM((8, TOK, A), BF16),
-            pltpu.VMEM((8, TOK, S), BF16),
+            pltpu.VMEM((8, TOK, AW), BF16),
+            pltpu.VMEM((8, TOK, SW), BF16),
             pltpu.VMEM((2, 8, TOK, D), BF16),
             pltpu.VMEM((4, 2, TOK, A), BF16),
             pltpu.VMEM((4, 2, TOK, S), BF16),
@@ -348,21 +351,22 @@
             pltpu.VMEM((2, 2, TOK, S), BF16),
             pltpu.VMEM((TOK, A), BF16),
             pltpu.VMEM((TOK, S), BF16),
-            pltpu.VMEM((NA + NS, GT, DH), BF16),
-            pltpu.VMEM((NA + NS, GT, DH), BF16),
-            pltpu.VMEM((NS, GT, DH), BF16),
-            pltpu.VMEM((NS, GT, DH), BF16),
-            pltpu.VMEM((NS, GT, DH), BF16),
-            pltpu.VMEM((NS, GT, DH), BF16),
+            pltpu.VMEM((NA, TA, DH), BF16),
+            pltpu.VMEM((NA, TA, DH), BF16),
+            pltpu.VMEM((NS, TS, DH), BF16),
+            pltpu.VMEM((NS, TS, DH), BF16),
+            pltpu.VMEM((NS, TS, DH), BF16),
+            pltpu.VMEM((NS, TS, DH), BF16),
+            pltpu.VMEM((NS, TS, DH), BF16),
+            pltpu.VMEM((NS, TS, DH), BF16),
             pltpu.VMEM((1, TOK), jnp.int32),
             pltpu.VMEM((1, 32), jnp.int32),
             pltpu.VMEM((TOK, D), BF16),
             dma((MESSAGES,)),
             dma((MESSAGES,)),
-            dma((NA + NS,)),
-            dma((NA + NS,)),
-            dma((NS,)),
-            dma((NS,)),
+            dma((2, NA)),
+            dma((2, NS)),
+            dma((2, NS)),
             dma((7,)),
         ],
         compiler_params=pltpu.CompilerParams(

time: 98.7 us -> 97.7 us (0.990)
  Pallas kernels: 97.8 us -> 96 us
    pallas_call x1, Pallas kernels: 94.4 us -> 92.6 us  [body(): pl.pallas_call(kernel, out_shape=(pltpu.VMEM((TOK, FF), BF16), pltpu.VMEM...]
where the time goes in v6:
time: 97.7 us; the launch traced here: 96.6 us
  Pallas kernels  96 us (98%)
    pallas_call x1, Pallas kernels, body(): pl.pallas_call(kernel, out_shape=(pltpu.VMEM((TOK, FF), BF16), pltpu.VMEM...  92.6 us
    pallas_call x1, Pallas kernels, body(): pl.pallas_call(write_out, out_shape=(jax.ShapeDtypeStruct((TOK, FF), BF16...  3.35 us

profile of v6, /device:TPU:2, one launch (start us, length us, event | category | flops | bytes accessed | tf_op | source)
XLA Modules:
  0.0 96.6 jit_solution(6456499527529118751)
XLA Ops:
  0.6 92.6 %shard_map.68 = (bf16[128,3584]{1,0:T(8,128)(2,1)S(1)}, f32[3584,512]{1,0:T(8,128)S(1)}) custom-call(bf16[128,3584]{1,0:T(8,128)(2,1)} %h_ref.1, bf16[128,1024]{1,0:T(8,128)(2,1)} %c_ref.1, s32[1,128]{1,0:T(1,128)} %bitcast.2, s32[1,32]{1,0:T(1,128)} %bitcast.3, bf16[3584,1024]{1,0:T(8,128)(2,1)} %w_ref.1), custom_call_target="tpu_custom_call" | custom-call | flops 15032385536 | bytes 25165824 | tf_op jit(solution)/shard_map/pallas_call | solution.py:334
  93.3 3.4 %shard_map.69 = (bf16[128,3584]{1,0:T(8,128)(2,1)}, f32[3584,512]{1,0:T(8,128)}) custom-call(bf16[128,3584]{1,0:T(8,128)(2,1)S(1)} %get-tuple-element.4.gh_ref, f32[3584,512]{1,0:T(8,128)S(1)} %get-tuple-element.5.gw_ref), custom_call_target="tpu_custom_call" | custom-call | tf_op jit(solution)/shard_map/pallas_call | solution.py:377

commit v7 on v6

--- a/solution.py
+++ b/solution.py
@@ -18,7 +18,7 @@
 FT = 512
 TA, TS = 256, 384
 NA, NS = AW // TA, SW // TS
-NW = 2
+NW = 4
 WR = S // 2 // NW
 MESSAGES = 96
 PIECES = 7
@@ -264,7 +264,6 @@
     give_back(NS - 1)
     terms_a(1, zp)
     terms_a(2, zm)
-    terms_a(3, z)
     w_dp = []
     for i in range(NW):
         got(w_x[i])
@@ -272,6 +271,7 @@
         w_dp.append(send(wx.at[rows, :], wx.at[rows, :], to_dp))
     got(*far_aq)
     near_aq = near(pa, ra2, ra1, q, A)
+    terms_a(3, z)
     got(*w_dp)
     terms_s(0, zo)
     far_sq = far(ps, rs2, q, S)
@@ -293,7 +293,7 @@
     own_tiles(ha, gsa, gra, sem_a, TA, 0, 0, 1)
     got(*near_sq)
     home(ps, rs1, q)
-    last_s = send(ps.at[3, q], rsx, to_x2)
+    last_s = send(ps.at[3, q], gh_ref.at[:, pl.ds(s_own, S)], to_x2)
     own_tiles(ha, gsa, gra, sem_a, TA, 0, 1, NA)
     own_sums(gsa, gra, sem_a, TA, 0, NA)
     own_sums(gss, grs, sem_s, TS, sw_own, NS)
@@ -305,11 +305,10 @@
     got(last_a)
     add(pa, (3, h), (rax, everything))
     gh_ref[:, 0:A] = pa[3, h]
-    got(last_s)
-    gh_ref[:, pl.ds(s_other, S)] = rsx[...]
     got(*near_sh)
     home(ps, rs1, h)
     gh_ref[:, pl.ds(s_own, S)] = ps[3, h]
+    got(last_s)
 
     for copy in sent:
         copy.wait_send()

time: 97.7 us -> 97.5 us (level)
  no operation moved by 1% of the time
where the time goes in v7:
time: 97.5 us; the launch traced here: 96.4 us
  Pallas kernels  95.8 us (98%)
    pallas_call x1, Pallas kernels, body(): pl.pallas_call(kernel, out_shape=(pltpu.VMEM((TOK, FF), BF16), pltpu.VMEM...  92.4 us
    pallas_call x1, Pallas kernels, body(): pl.pallas_call(write_out, out_shape=(jax.ShapeDtypeStruct((TOK, FF), BF16...  3.35 us

profile of v7, /device:TPU:2, one launch (start us, length us, event | category | flops | bytes accessed | tf_op | source)
XLA Modules:
  0.0 96.4 jit_solution(424836496929780316)
XLA Ops:
  0.6 92.4 %shard_map.68 = (bf16[128,3584]{1,0:T(8,128)(2,1)S(1)}, f32[3584,512]{1,0:T(8,128)S(1)}) custom-call(bf16[128,3584]{1,0:T(8,128)(2,1)} %h_ref.1, bf16[128,1024]{1,0:T(8,128)(2,1)} %c_ref.1, s32[1,128]{1,0:T(1,128)} %bitcast.2, s32[1,32]{1,0:T(1,128)} %bitcast.3, bf16[3584,1024]{1,0:T(8,128)(2,1)} %w_ref.1), custom_call_target="tpu_custom_call" | custom-call | flops 15032385536 | bytes 25165824 | tf_op jit(solution)/shard_map/pallas_call | solution.py:333
  93.0 3.4 %shard_map.69 = (bf16[128,3584]{1,0:T(8,128)(2,1)}, f32[3584,512]{1,0:T(8,128)}) custom-call(bf16[128,3584]{1,0:T(8,128)(2,1)S(1)} %get-tuple-element.4.gh_ref, f32[3584,512]{1,0:T(8,128)S(1)} %get-tuple-element.5.gw_ref), custom_call_target="tpu_custom_call" | custom-call | tf_op jit(solution)/shard_map/pallas_call | solution.py:376

commit v8 on v7

--- a/solution.py
+++ b/solution.py
@@ -302,6 +302,10 @@
     for j in range(NS):
         got(returns[j])
         gw_ref[pl.ds(pl.multiple_of(sw_other + j * TS, 128), TS), :] = xin[j].astype(F32)
+    late = [*near_ah, *near_sh, last_a, last_s]
+    for copy in sent:
+        if all(copy is not other for other in late):
+            copy.wait_send()
     got(last_a)
     add(pa, (3, h), (rax, everything))
     gh_ref[:, 0:A] = pa[3, h]
@@ -310,7 +314,7 @@
     gh_ref[:, pl.ds(s_own, S)] = ps[3, h]
     got(last_s)
 
-    for copy in sent:
+    for copy in late:
         copy.wait_send()
 
 

time: 97.5 us -> 97.4 us (level)
  no operation moved by 1% of the time
where the time goes in v8:
time: 97.4 us; the launch traced here: 96.3 us
  Pallas kernels  95.7 us (98%)
    pallas_call x1, Pallas kernels, body(): pl.pallas_call(kernel, out_shape=(pltpu.VMEM((TOK, FF), BF16), pltpu.VMEM...  92.3 us
    pallas_call x1, Pallas kernels, body(): pl.pallas_call(write_out, out_shape=(jax.ShapeDtypeStruct((TOK, FF), BF16...  3.35 us

profile of v8, /device:TPU:2, one launch (start us, length us, event | category | flops | bytes accessed | tf_op | source)
XLA Modules:
  0.0 96.3 jit_solution(2627698547728502849)
XLA Ops:
  0.6 92.3 %shard_map.68 = (bf16[128,3584]{1,0:T(8,128)(2,1)S(1)}, f32[3584,512]{1,0:T(8,128)S(1)}) custom-call(bf16[128,3584]{1,0:T(8,128)(2,1)} %h_ref.1, bf16[128,1024]{1,0:T(8,128)(2,1)} %c_ref.1, s32[1,128]{1,0:T(1,128)} %bitcast.2, s32[1,32]{1,0:T(1,128)} %bitcast.3, bf16[3584,1024]{1,0:T(8,128)(2,1)} %w_ref.1), custom_call_target="tpu_custom_call" | custom-call | flops 15032385536 | bytes 25165824 | tf_op jit(solution)/shard_map/pallas_call | solution.py:337
  92.9 3.4 %shard_map.69 = (bf16[128,3584]{1,0:T(8,128)(2,1)}, f32[3584,512]{1,0:T(8,128)}) custom-call(bf16[128,3584]{1,0:T(8,128)(2,1)S(1)} %get-tuple-element.4.gh_ref, f32[3584,512]{1,0:T(8,128)S(1)} %get-tuple-element.5.gw_ref), custom_call_target="tpu_custom_call" | custom-call | tf_op jit(solution)/shard_map/pallas_call | solution.py:380
